TPU v7x, 256 devices: a whole 4x4x8 slice. The times are simulated.
256 devices in a mesh: gx: 16 (over x_hi, y, core), gy: 16 (over z, x_lo).
Axes of the slice: x: 4 (x_hi: 2, x_lo: 2; x = x_hi * 2 + x_lo), y: 4, z: 8, core: 2. Of those that a mesh axis runs over, the one named last changes fastest.
Arguments:
- inputs: bfloat16 [64, 64, 14, 256], P('gx', 'gy'), may hold values from -6 to 6
- cotangent: bfloat16 [64, 64, 8, 256], P('gx', 'gy'), may hold values from -6 to 6
- w_qkv: bfloat16 [256, 768], replicated, may hold values from -0.375 to 0.375
- w_out: bfloat16 [256, 256], replicated, may hold values from -0.375 to 0.375
Outputs:
- grad_inputs: bfloat16 [64, 64, 14, 256], P('gx', 'gy')
- grad_wqkv: float32 [256, 768], replicated
- grad_wout: float32 [256, 256], replicated
All inputs are finite; a program needn't handle non-finite values.
Results may differ from a plain program's by a relative error of at most 0.012.
Values may be sent and summed in bfloat16 or wider, within the bound.
No kernel may reach another device: no remote copies, remote signals or barrier semaphores. Data moves between devices by JAX's collectives and lax.ppermute only.
A program may use at most 64 MiB of HBM per device.

v0:
```python
import jax
import jax.numpy as jnp
from jax import lax
from jax.sharding import PartitionSpec as P

H = 4
HD = 64
RADIUS = 3


def extended(shard, sides, width):
    for axis, dim in sides:
        size, length = (lax.axis_size(axis), shard.shape[dim])
        up = [(i, (i + 1) % size) for i in range(size)]
        down = [(j, i) for i, j in up]
        last = lax.slice_in_dim(shard, length - width, length, axis=dim)
        leading = lax.slice_in_dim(shard, 0, width, axis=dim)
        before = lax.ppermute(last, axis, up)
        after = lax.ppermute(leading, axis, down)
        shard = jnp.concatenate([before, shard, after], axis=dim)
    return shard


def passed_along(block, axis, distance):
    devices = range(lax.axis_size(axis))
    route = [((i - distance) % len(devices), i) for i in devices]
    return lax.ppermute(block, axis, route)


def split_rims(field, dim):
    count = field.shape[dim] - 2 * RADIUS
    lower_rim = lax.slice_in_dim(field, 0, RADIUS, axis=dim)
    middle = lax.slice_in_dim(field, RADIUS, RADIUS + count, axis=dim)
    upper_rim = lax.slice_in_dim(field, RADIUS + count, count + 2 * RADIUS, axis=dim)
    return (lower_rim, middle, upper_rim)


def add_edges(middle, from_below, from_above, dim):
    count = middle.shape[dim]
    head_part = lax.slice_in_dim(middle, 0, RADIUS, axis=dim) + from_below
    middle = lax.dynamic_update_slice_in_dim(middle, head_part, 0, dim)
    tail_part = lax.slice_in_dim(middle, count - RADIUS, count, axis=dim) + from_above
    return lax.dynamic_update_slice_in_dim(middle, tail_part, count - RADIUS, dim)


def body(inputs, cotangent, w_qkv, w_out):
    rows_x, rows_y, planes, channels = cotangent.shape
    ext_planes = inputs.shape[2]
    wide_y = rows_y + 2 * RADIUS
    window_len = 2 * RADIUS + 1
    score_scale = HD ** (-0.5)
    highest = lax.Precision.HIGHEST
    query_cells = rows_y * planes
    key_cells = wide_y * ext_planes
    inner_in = inputs[:, :, RADIUS : RADIUS + planes]
    query = jnp.dot(
        inner_in.reshape(-1, channels), w_qkv[:, :channels], preferred_element_type=jnp.float32
    )
    query = query.astype(jnp.bfloat16).reshape(rows_x, query_cells, H, HD)
    local_kv = jnp.dot(
        inputs.reshape(-1, channels), w_qkv[:, channels:], preferred_element_type=jnp.float32
    )
    local_kv = local_kv.astype(jnp.bfloat16).reshape(rows_x, rows_y, ext_planes, 2 * channels)
    keyval = extended(local_kv, (("gx", 0), ("gy", 1)), RADIUS)
    grad_attn = jnp.dot(
        cotangent.reshape(-1, channels), w_out.T, preferred_element_type=jnp.float32
    )
    grad_attn = grad_attn.astype(jnp.bfloat16).reshape(rows_x, query_cells, H, HD)
    steps_x = jnp.arange(window_len, dtype=jnp.int32)
    query_index = jnp.arange(query_cells, dtype=jnp.int32)
    key_index = jnp.arange(key_cells, dtype=jnp.int32)
    reach_y = key_index[None, :] // ext_planes - query_index[:, None] // planes
    reach_z = key_index[None, :] % ext_planes - query_index[:, None] % planes
    inside = (reach_y >= 0) & (reach_y <= 2 * RADIUS) & (reach_z >= 0) & (reach_z <= 2 * RADIUS)

    def slab_at(step_x):
        key_slab = lax.dynamic_slice_in_dim(keyval, step_x, rows_x, 0).reshape(
            rows_x, key_cells, 2 * channels
        )
        keys_all = key_slab[..., :channels].reshape(rows_x, key_cells, H, HD)
        vals_all = key_slab[..., channels:].reshape(rows_x, key_cells, H, HD)
        return (keys_all, vals_all)

    def exps_at(keys_all):
        scores = (
            jnp.einsum("xqhd,xkhd->xhqk", query, keys_all, preferred_element_type=jnp.float32)
            * score_scale
        )
        return jnp.where(inside, jnp.exp(scores), 0.0)

    def total_pass(total, step_x):
        keys_all = slab_at(step_x)[0]
        return (total + jnp.sum(exps_at(keys_all), axis=-1), jnp.zeros((), jnp.float32))

    total = lax.scan(total_pass, jnp.zeros((rows_x, H, query_cells), jnp.float32), steps_x)[0]

    def probs_at(step_x):
        keys_all, vals_all = slab_at(step_x)
        probs = exps_at(keys_all) / total[..., None]
        grad_probs = jnp.einsum(
            "xqhd,xkhd->xhqk", grad_attn, vals_all, preferred_element_type=jnp.float32
        )
        return (keys_all, vals_all, probs, probs.astype(jnp.bfloat16), grad_probs)

    def value_pass(state, step_x):
        summed, balance = state
        vals_all, probs, prob_bf, grad_probs = probs_at(step_x)[1:]
        summed = summed + jnp.einsum(
            "xhqk,xkhd->xqhd", prob_bf, vals_all, preferred_element_type=jnp.float32
        )
        balance = balance + jnp.sum(probs * grad_probs, axis=-1)
        return ((summed, balance), jnp.zeros((), jnp.float32))

    start_state = (
        jnp.zeros((rows_x, query_cells, H, HD), jnp.float32),
        jnp.zeros((rows_x, H, query_cells), jnp.float32),
    )
    attn_sum, balance = lax.scan(value_pass, start_state, steps_x)[0]
    attended = attn_sum.astype(jnp.bfloat16).reshape(-1, channels)
    grad_wout_part = jnp.dot(
        attended.T, cotangent.reshape(-1, channels), preferred_element_type=jnp.float32
    )

    def key_pass(state, step_x):
        grad_query, grad_grown = state
        keys_all, vals_all, probs, prob_bf, grad_probs = probs_at(step_x)
        grad_scores = (probs * (grad_probs - balance[..., None]) * score_scale).astype(jnp.bfloat16)
        grad_query = grad_query + jnp.einsum(
            "xhqk,xkhd->xqhd", grad_scores, keys_all, preferred_element_type=jnp.float32
        )
        key_term = jnp.einsum(
            "xhqk,xqhd->xkhd", grad_scores, query, preferred_element_type=jnp.float32
        )
        value_term = jnp.einsum(
            "xhqk,xqhd->xkhd", prob_bf, grad_attn, preferred_element_type=jnp.float32
        )
        frame = jnp.concatenate(
            [
                key_term.reshape(rows_x, key_cells, channels),
                value_term.reshape(rows_x, key_cells, channels),
            ],
            axis=-1,
        )
        frame = frame.reshape(rows_x, wide_y, ext_planes, 2 * channels)
        current = lax.dynamic_slice_in_dim(grad_grown, step_x, rows_x, 0)
        grad_grown = lax.dynamic_update_slice_in_dim(grad_grown, current + frame, step_x, 0)
        return ((grad_query, grad_grown), jnp.zeros((), jnp.float32))

    initial = (
        jnp.zeros((rows_x, query_cells, H, HD), jnp.float32),
        jnp.zeros((rows_x + 2 * RADIUS, wide_y, ext_planes, 2 * channels), jnp.float32),
    )
    finals = lax.scan(key_pass, initial, steps_x)[0]
    grad_query = jnp.pad(
        finals[0].reshape(rows_x, rows_y, planes, channels),
        ((0, 0), (0, 0), (RADIUS, RADIUS), (0, 0)),
    )
    grad_grown = finals[1]
    lower_rim, middle, upper_rim = split_rims(grad_grown, 0)
    middle = add_edges(
        middle,
        passed_along(upper_rim.astype(jnp.bfloat16), "gx", 1).astype(upper_rim.dtype),
        passed_along(lower_rim.astype(jnp.bfloat16), "gx", -1).astype(lower_rim.dtype),
        0,
    )
    lower_rim, middle, upper_rim = split_rims(middle, 1)
    grad_keyval = add_edges(
        middle,
        passed_along(upper_rim.astype(jnp.bfloat16), "gy", 1).astype(upper_rim.dtype),
        passed_along(lower_rim.astype(jnp.bfloat16), "gy", -1).astype(lower_rim.dtype),
        1,
    )
    grad_hidden = jnp.concatenate([grad_query, grad_keyval], axis=-1).reshape(-1, 3 * channels)
    grad_inputs = jnp.dot(grad_hidden, w_qkv.astype(jnp.float32).T, precision=highest)
    grad_inputs = grad_inputs.reshape(rows_x, rows_y, ext_planes, channels)
    grad_wqkv_part = jnp.dot(
        inputs.reshape(-1, channels).astype(jnp.float32).T, grad_hidden, precision=highest
    )
    totals = lax.psum((grad_wqkv_part, grad_wout_part), ("gx", "gy"))
    return (grad_inputs.astype(jnp.bfloat16), totals[0], totals[1])


def solution(mesh):
    placed = (P("gx", "gy", None, None), P("gx", "gy", None, None), P(), P())
    return jax.shard_map(
        body,
        mesh=mesh,
        in_specs=placed,
        out_specs=(P("gx", "gy", None, None), P(), P()),
        check_vma=False,
    )
```

profile of v0, /device:TPU:1, one launch (start us, length us, event | category | flops | bytes accessed | tf_op | source)
XLA Modules:
  0.0 594.3 jit_solution(4388820096405433341)
XLA Ops:
  9.5 2.8 collective-permute-start
  13.5 1.4 collective-permute-done
  14.9 2.6 collective-permute-done.1
  18.4 1.5 collective-permute-start.2
  19.9 5.3 collective-permute-start.3
  26.4 13.9 %collective-permute-done.2 = bf16[10,3,14,512]{3,2,1,0:T(8,128)(2,1)S(1)} collective-permute-done((bf16[10,3,14,512]{3,2,1,0:T(8,128)(2,1)}, bf16[10,3,14,512]{3,2,1,0:T(8,128)(2,1)S(1)}, u32[]{:S(2)}, u32[]{:S(2)}) %collective-permute-start.2) | collective-permute-done | bytes 430112 | tf_op jit(solution)/shard_map/ppermute | solution.py:18
  40.7 2.4 copy.36
  43.2 37.7 %while.37 = (s32[]{:T(128)}, f32[4,4,32]{2,1,0:T(4,128)S(1)}, s32[7]{0:T(128)S(1)}, bf16[10,10,14,512]{3,0,2,1:T(8,128)(2,1)}, bf16[4,32,4,64]{3,1,2,0:T(8,128)(...) while((s32[]{:T(128)}, f32[4,4,32]{2,1,0:T(4,128)S(1)}, ...), condition=%wide.region_2.3_spmd.clone, body=%wide.region_0.2_spmd.clone.sunk | while | flops 9430918 | bytes 2664729 | solution.py:95
  45.8 2.0 constant_dynamic-slice_fusion.6
  51.2 2.0 constant_dynamic-slice_fusion.6
  56.6 2.0 constant_dynamic-slice_fusion.6
  61.9 2.0 constant_dynamic-slice_fusion.6
  67.3 2.0 constant_dynamic-slice_fusion.6
  72.7 2.0 constant_dynamic-slice_fusion.6
  78.1 2.0 constant_dynamic-slice_fusion.6
  80.9 44.0 %while.38 = (s32[]{:T(128)}, f32[4,32,4,64]{3,1,2,0:T(8,128)S(1)}, f32[4,4,32]{2,1,0:T(4,128)S(1)}, s32[7]{0:T(128)S(1)}, bf16[10,10,14,512]{3,0,2,1:T(8,128)(2,...) while((s32[]{:T(128)}, f32[4,32,4,64]{3,1,2,0:T(8,128)S(1)}, ...), condition=%wide.region_5.6_spmd.clone, body=%wide.region_3.5_spmd.clone.sunk | while | flops 28061572 | bytes 5574962 | solution.py:118
  83.5 2.0 constant_dynamic-slice_fusion.7
  89.8 2.0 constant_dynamic-slice_fusion.7
  96.1 2.0 constant_dynamic-slice_fusion.7
  102.4 2.0 constant_dynamic-slice_fusion.7
  108.7 2.0 constant_dynamic-slice_fusion.7
  114.9 2.0 constant_dynamic-slice_fusion.7
  121.2 2.0 constant_dynamic-slice_fusion.7
  124.9 2.7 broadcast_in_dim.30
  127.6 166.5 %while.39 = (s32[]{:T(128)}, f32[4,32,4,64]{3,1,2,0:T(8,128)}, f32[10,10,14,512]{3,0,2,1:T(8,128)}, s32[7]{0:T(128)S(1)}, bf16[10,10,14,512]{3,0,2,1:T(8,128)(2,...) while((s32[]{:T(128)}, f32[4,32,4,64]{3,1,2,0:T(8,128)}, ...), condition=%wide.region_7.8_spmd.clone, body=%wide.region_6.7_spmd.clone.sunk | while | flops 47127940 | bytes 17598784 | solution.py:153
  130.2 2.0 constant_dynamic-slice_fusion.8
  138.5 2.9 maximum_add_fusion.2
  141.5 9.1 %dynamic_update_slice.25 = f32[10,10,14,512]{3,0,2,1:T(8,128)} dynamic-update-slice(f32[10,10,14,512]{3,0,2,1:T(8,128)} %get-tuple-element.746, f32[4,10,14,512]{3,0,2,1:T(4,128)S(1)} %maximum_add_fusion.2, s32[]{:T(128)S(6)} %select_n.114, s32[]{:T(128)} %constant.85.clone.1..sunk.2, s32[]{:T(128)} %constant.85.clone.1..sunk.2, s32[]{:T(128)} %constant.85.clone.1..sunk.2) | dynamic-update-slice | bytes 2293764 | tf_op jit(solution)/shard_map/while/body/eval_jaxpr/dynamic_update_slice | solution.py:146
  153.2 2.0 constant_dynamic-slice_fusion.8
  156.4 1.9 fusion.146
  162.5 2.9 maximum_add_fusion.2
  165.4 9.1 %dynamic_update_slice.25 = f32[10,10,14,512]{3,0,2,1:T(8,128)} dynamic-update-slice(f32[10,10,14,512]{3,0,2,1:T(8,128)} %get-tuple-element.746, f32[4,10,14,512]{3,0,2,1:T(4,128)S(1)} %maximum_add_fusion.2, s32[]{:T(128)S(6)} %select_n.114, s32[]{:T(128)} %constant.85.clone.1..sunk.2, s32[]{:T(128)} %constant.85.clone.1..sunk.2, s32[]{:T(128)} %constant.85.clone.1..sunk.2) | dynamic-update-slice | bytes 2293764 | tf_op jit(solution)/shard_map/while/body/eval_jaxpr/dynamic_update_slice | solution.py:146
  177.1 2.0 constant_dynamic-slice_fusion.8
  180.3 1.9 fusion.146
  186.4 2.9 maximum_add_fusion.2
  189.3 9.1 %dynamic_update_slice.25 = f32[10,10,14,512]{3,0,2,1:T(8,128)} dynamic-update-slice(f32[10,10,14,512]{3,0,2,1:T(8,128)} %get-tuple-element.746, f32[4,10,14,512]{3,0,2,1:T(4,128)S(1)} %maximum_add_fusion.2, s32[]{:T(128)S(6)} %select_n.114, s32[]{:T(128)} %constant.85.clone.1..sunk.2, s32[]{:T(128)} %constant.85.clone.1..sunk.2, s32[]{:T(128)} %constant.85.clone.1..sunk.2) | dynamic-update-slice | bytes 2293764 | tf_op jit(solution)/shard_map/while/body/eval_jaxpr/dynamic_update_slice | solution.py:146
  201.0 2.0 constant_dynamic-slice_fusion.8
  204.3 1.9 fusion.146
  210.3 2.9 maximum_add_fusion.2
  213.2 9.1 %dynamic_update_slice.25 = f32[10,10,14,512]{3,0,2,1:T(8,128)} dynamic-update-slice(f32[10,10,14,512]{3,0,2,1:T(8,128)} %get-tuple-element.746, f32[4,10,14,512]{3,0,2,1:T(4,128)S(1)} %maximum_add_fusion.2, s32[]{:T(128)S(6)} %select_n.114, s32[]{:T(128)} %constant.85.clone.1..sunk.2, s32[]{:T(128)} %constant.85.clone.1..sunk.2, s32[]{:T(128)} %constant.85.clone.1..sunk.2) | dynamic-update-slice | bytes 2293764 | tf_op jit(solution)/shard_map/while/body/eval_jaxpr/dynamic_update_slice | solution.py:146
  224.9 2.0 constant_dynamic-slice_fusion.8
  228.2 1.9 fusion.146
  234.2 2.9 maximum_add_fusion.2
  237.2 9.1 %dynamic_update_slice.25 = f32[10,10,14,512]{3,0,2,1:T(8,128)} dynamic-update-slice(f32[10,10,14,512]{3,0,2,1:T(8,128)} %get-tuple-element.746, f32[4,10,14,512]{3,0,2,1:T(4,128)S(1)} %maximum_add_fusion.2, s32[]{:T(128)S(6)} %select_n.114, s32[]{:T(128)} %constant.85.clone.1..sunk.2, s32[]{:T(128)} %constant.85.clone.1..sunk.2, s32[]{:T(128)} %constant.85.clone.1..sunk.2) | dynamic-update-slice | bytes 2293764 | tf_op jit(solution)/shard_map/while/body/eval_jaxpr/dynamic_update_slice | solution.py:146
  248.8 2.0 constant_dynamic-slice_fusion.8
  252.1 1.9 fusion.146
  258.1 2.9 maximum_add_fusion.2
  261.1 9.1 %dynamic_update_slice.25 = f32[10,10,14,512]{3,0,2,1:T(8,128)} dynamic-update-slice(f32[10,10,14,512]{3,0,2,1:T(8,128)} %get-tuple-element.746, f32[4,10,14,512]{3,0,2,1:T(4,128)S(1)} %maximum_add_fusion.2, s32[]{:T(128)S(6)} %select_n.114, s32[]{:T(128)} %constant.85.clone.1..sunk.2, s32[]{:T(128)} %constant.85.clone.1..sunk.2, s32[]{:T(128)} %constant.85.clone.1..sunk.2) | dynamic-update-slice | bytes 2293764 | tf_op jit(solution)/shard_map/while/body/eval_jaxpr/dynamic_update_slice | solution.py:146
  272.7 2.0 constant_dynamic-slice_fusion.8
  276.0 1.9 fusion.146
  282.0 2.9 maximum_add_fusion.2
  285.0 9.1 %dynamic_update_slice.25 = f32[10,10,14,512]{3,0,2,1:T(8,128)} dynamic-update-slice(f32[10,10,14,512]{3,0,2,1:T(8,128)} %get-tuple-element.746, f32[4,10,14,512]{3,0,2,1:T(4,128)S(1)} %maximum_add_fusion.2, s32[]{:T(128)S(6)} %select_n.114, s32[]{:T(128)} %constant.85.clone.1..sunk.2, s32[]{:T(128)} %constant.85.clone.1..sunk.2, s32[]{:T(128)} %constant.85.clone.1..sunk.2) | dynamic-update-slice | bytes 2293764 | tf_op jit(solution)/shard_map/while/body/eval_jaxpr/dynamic_update_slice | solution.py:146
  294.0 4.0 fusion.57
  299.2 3.3 collective-permute-start.4
  303.7 1.8 copy.39
  306.9 1.7 collective-permute-done.4
  308.6 1.2 fusion.38
  309.8 1.5 collective-permute-done.5
  311.3 1.3 fusion.37
  314.5 5.2 collective-permute-start.7
  319.6 1.5 collective-permute-done.6
  322.4 1.7 convolution_bitcast_fusion.5
  325.4 259.1 %all-reduce.4.cloned.1.call-done = (f32[256,768]{0,1:T(8,128)}, f32[256,256]{1,0:T(8,128)}) async-done(((f32[256,768]{0,1:T(8,128)}, f32[256,256]{1,0:T(8,128)}), (f32[256,768]{0,1:T(8,128)}, f32[256,256]{1,0:T(8,128)})) %all-reduce.4.cloned.1.call-update) | async-done | bytes 1048592 | tf_op jit(solution)/shard_map/psum | solution.py:179
  584.5 2.3 copy.46
  (265 shorter events, 82.3 us)
Async XLA Ops:
  7.2 5.9 copy-start
  7.2 5.9 copy-start.6
  7.2 577.3 %all-reduce.4.cloned.1.call-start = ((), (), s32[]{:S(2)}) async-start(), calls=%async_computation | async-start | bytes 2097152 | tf_op jit(solution)/shard_map/psum | solution.py:179
  9.5 5.4 collective-permute-start
  12.3 5.2 collective-permute-start.1
  18.4 21.9 %collective-permute-start.2 = (bf16[10,3,14,512]{3,2,1,0:T(8,128)(2,1)}, bf16[10,3,14,512]{3,2,1,0:T(8,128)(2,1)S(1)}, u32[]{:S(2)}, u32[]{:S(2)}) collective-permute-start(bf16[10,3,14,512]{3,2,1,0:T(8,128)(2,1)} %get-tuple-element.424), channel_id=1, source_target_pairs={{0,1},{1,2},{2,3},{3,4},{4,5},{5,6},{6,7},{7,8},{8,9},{9,10},{10,1... | collective-permute-start | bytes 1290248 | tf_op jit(solution)/shard_map/ppermute | solution.py:18
  19.9 20.6 %collective-permute-start.3 = (bf16[10,3,14,512]{3,2,1,0:T(8,128)(2,1)S(1)}, bf16[10,3,14,512]{3,2,1,0:T(8,128)(2,1)S(1)}, u32[]{:S(2)}, u32[]{:S(2)}) collective-permute-start(bf16[10,3,14,512]{3,2,1,0:T(8,128)(2,1)S(1)} %get-tuple-element.425), channel_id=1, source_target_pairs={{1,0},{2,1},{3,2},{4,3},{5,4},{6,5},{7,6},{8,7},{9,8},{10,9},{11,1... | collective-permute-start | bytes 1290248 | tf_op jit(solution)/shard_map/ppermute | solution.py:19
  124.9 2.7 copy-start.1
  298.1 4.8 copy-start.2
  299.2 9.4 %collective-permute-start.4 = (bf16[3,10,14,512]{3,2,1,0:T(8,128)(2,1)}, bf16[3,10,14,512]{3,2,1,0:T(8,128)(2,1)}, u32[]{:S(2)}, u32[]{:S(2)}) collective-permute-start(bf16[3,10,14,512]{3,2,1,0:T(8,128)(2,1)} %get-tuple-element.421), channel_id=1, source_target_pairs={{240,0},{0,16},{16,32},{32,48},{48,64},{64,80},{80,96},{96,112},{1... | collective-permute-start | bytes 1290248 | tf_op jit(solution)/shard_map/ppermute | solution.py:27
  302.5 8.9 %collective-permute-start.5 = (bf16[3,10,14,512]{3,2,1,0:T(8,128)(2,1)}, bf16[3,10,14,512]{3,2,1,0:T(8,128)(2,1)}, u32[]{:S(2)}, u32[]{:S(2)}) collective-permute-start(bf16[3,10,14,512]{3,2,1,0:T(8,128)(2,1)} %get-tuple-element.420), channel_id=1, source_target_pairs={{16,0},{32,16},{48,32},{64,48},{80,64},{96,80},{112,96},{128,112},... | collective-permute-start | bytes 1290248 | tf_op jit(solution)/shard_map/ppermute | solution.py:27
  312.6 0.8 copy-start.5
  312.7 0.9 copy-start.7
  312.8 9.5 %copy-start.8 = (bf16[4,4,14,256]{3,1,2,0:T(4,128)(2,1)S(1)}, bf16[4,4,14,256]{3,1,2,0:T(4,128)(2,1)}, u32[]{:S(2)}) copy-start(bf16[4,4,14,256]{3,1,2,0:T(4,128)(2,1)} %param.10) | copy-start | bytes 344068
  312.8 8.3 %collective-permute-start.6 = (bf16[4,3,14,512]{3,2,1,0:T(8,128)(2,1)S(1)}, bf16[4,3,14,512]{3,2,1,0:T(8,128)(2,1)S(1)}, u32[]{:S(2)}, u32[]{:S(2)}) collective-permute-start(bf16[4,3,14,512]{3,2,1,0:T(8,128)(2,1)S(1)} %get-tuple-element.423), channel_id=1, source_target_pairs={{15,0},{0,1},{1,2},{2,3},{3,4},{4,5},{5,6},{6,7},{7,8},{8,9},{9,10... | collective-permute-start | bytes 516104 | tf_op jit(solution)/shard_map/ppermute | solution.py:27
  314.5 7.8 %collective-permute-start.7 = (bf16[4,3,14,512]{3,2,1,0:T(8,128)(2,1)S(1)}, bf16[4,3,14,512]{3,2,1,0:T(8,128)(2,1)S(1)}, u32[]{:S(2)}, u32[]{:S(2)}) collective-permute-start(bf16[4,3,14,512]{3,2,1,0:T(8,128)(2,1)S(1)} %get-tuple-element.422), channel_id=1, source_target_pairs={{1,0},{2,1},{3,2},{4,3},{5,4},{6,5},{7,6},{8,7},{9,8},{10,9},{11,1... | collective-permute-start | bytes 516104 | tf_op jit(solution)/shard_map/ppermute | solution.py:27
  322.4 1.7 copy-start.3
  584.4 2.3 copy-start.4
Sparse Core Ops, SparseCore 0:
  324.2 260.1 all-reduce.3
where the time goes:
time: 598 us; the launch traced here: 594 us
  waiting for transfers between devices  283 us (47%)
  local copies, waits for them, and re-layouts  172 us (29%)
  loops' own time  42.1 us (7%)
  matrix products  34.4 us (6%)
  other arithmetic  29.6 us (5%)
  starting transfers between devices  19.2 us (3%)
  between operations  14.4 us (2%)
    psum x1, waiting for transfers between devices, body(): totals = lax.psum((grad_wqkv_part, grad_wout_part), ('gx', 'gy'))  259 us
    dynamic_update_slice x7, local copies, waits for them, and re-layouts, key_pass(): lax.dynamic_update_slice_in_dim(grad_grown, current + frame, step_x, 0)  63.4 us
    dynamic_slice x21, local copies, waits for them, and re-layouts, slab_at(): lax.dynamic_slice_in_dim(keyval, step_x, rows_x, 0)  42.7 us
    add x7, other arithmetic, key_pass(): current + frame  20.6 us
    ppermute x2, waiting for transfers between devices, extended(): before = lax.ppermute(last, axis, up)  15.3 us
    another operation x1, loops' own time, body(): finals = lax.scan(key_pass, initial, steps_x)[0]  14.2 us
    another operation x1, loops' own time, body(): attn_sum, balance = lax.scan(value_pass, start_state, steps_x)[0]  14.1 us
    another operation x1, loops' own time, body(): lax.scan(total_pass, jnp.zeros((rows_x, H, query_cells), jnp.float32), st...  13.9 us
  transfers between devices with their start and end apart: 9, of which 9 were waited for; matrix products, arithmetic and copies ran while one was open for 2% of the time, Pallas kernels for 0%

commit v1 on v0

v1 whole, which is shorter than its diff:
```python
import jax
import jax.numpy as jnp
from jax import lax
from jax.experimental import pallas as pl
from jax.experimental.pallas import tpu as pltpu
from jax.sharding import Mesh, PartitionSpec as P

H = 4
HD = 64
C = H * HD
RADIUS = 3
CELLS = 4
WIDE = CELLS + 2 * RADIUS
Z = 8
ZE = 14
ZP = 16
ROWS = WIDE * ZP
KEYS = WIDE * ROWS
QUERIES = CELLS * CELLS * Z
LANES = H * QUERIES
FAR = -1e30

NT = (((1,), (1,)), ((), ()))
TN = (((0,), (0,)), ((), ()))
F32 = jnp.float32
BF16 = jnp.bfloat16


def mm(a, b, dims=(((1,), (0,)), ((), ()))):
    return lax.dot_general(a, b, dims, preferred_element_type=F32)


def local_kernel(
    own, ylo, yhi, xlo, xhi, cot, wqkv, wout,
    grad_lo, grad_mid, grad_hi, dw,
    xs, ks, vs, qbd, gabd, es, gps, pbs, dss, gkvs,
):
    xs[...] = jnp.zeros_like(xs)
    xs[0:RADIUS, :, 0:ZE, :] = xlo[...]
    xs[RADIUS + CELLS :, :, 0:ZE, :] = xhi[...]
    xs[RADIUS : RADIUS + CELLS, 0:RADIUS, 0:ZE, :] = ylo[...]
    xs[RADIUS : RADIUS + CELLS, RADIUS : RADIUS + CELLS, 0:ZE, :] = own[...]
    xs[RADIUS : RADIUS + CELLS, RADIUS + CELLS :, 0:ZE, :] = yhi[...]

    inner = own[...].astype(F32)[:, :, RADIUS : RADIUS + Z, :].reshape(QUERIES, C).astype(BF16)
    cot2 = cot[...].astype(F32).reshape(QUERIES, C).astype(BF16)
    query = mm(inner, wqkv[:, :C]).astype(BF16).astype(F32) * HD ** (-0.5)
    grad_attn = mm(cot2, wout[...], NT).astype(BF16).astype(F32)
    head = lax.broadcasted_iota(jnp.int32, (QUERIES, C), 1) // HD
    for h in range(H):
        rows = slice(h * QUERIES, (h + 1) * QUERIES)
        qbd[rows, :] = jnp.where(head == h, query, 0.0).astype(BF16)
        gabd[rows, :] = jnp.where(head == h, grad_attn, 0.0).astype(BF16)

    lane = lax.broadcasted_iota(jnp.int32, (1, QUERIES), 1)
    query_x = lane // (CELLS * Z)
    query_y = lane // Z % CELLS
    query_z = lax.broadcasted_iota(jnp.int32, (ZP, QUERIES), 1) % Z

    def outside(step):
        return jnp.where((step >= 0) & (step <= 2 * RADIUS), 0.0, FAR)

    far_z = outside(lax.broadcasted_iota(jnp.int32, (ZP, QUERIES), 0) - query_z)
    far_yz = [far_z + outside(ky - query_y) for ky in range(WIDE)]

    total = jnp.zeros((8, LANES), F32)
    weighted = jnp.zeros((8, LANES), F32)
    for kx in range(WIDE):
        rows = slice(kx * ROWS, (kx + 1) * ROWS)
        kv = mm(xs[kx].reshape(ROWS, C), wqkv[:, C:]).astype(BF16)
        ks[rows, :] = kv[:, :C]
        vs[rows, :] = kv[:, C:]
        far_x = outside(kx - query_x)
        far = jnp.concatenate([part + far_x for part in far_yz], axis=0)
        scores = mm(kv[:, :C], qbd[...], NT) + jnp.concatenate([far] * H, axis=1)
        exps = jnp.exp(scores)
        grad_probs = mm(kv[:, C:], gabd[...], NT)
        es[rows, :] = exps
        gps[rows, :] = grad_probs
        total += jnp.sum(exps.reshape(ROWS // 8, 8, LANES), axis=0)
        weighted += jnp.sum((exps * grad_probs).reshape(ROWS // 8, 8, LANES), axis=0)

    inverse = 1.0 / jnp.sum(total, axis=0, keepdims=True)
    balance = jnp.sum(weighted, axis=0, keepdims=True) * inverse

    for kx in range(WIDE):
        rows = slice(kx * ROWS, (kx + 1) * ROWS)
        probs = es[rows, :] * inverse
        prob_bf = probs.astype(BF16)
        slopes = (probs * (gps[rows, :] - balance)).astype(BF16)
        pbs[rows, :] = prob_bf
        dss[rows, :] = slopes
        grad_kv = jnp.concatenate(
            [mm(slopes, qbd[...]).astype(BF16), mm(prob_bf, gabd[...]).astype(BF16)], axis=1
        )
        gkvs[rows, :] = grad_kv
        grad_in = mm(grad_kv, wqkv[:, C:], NT).reshape(WIDE, ZP, C)
        if kx < RADIUS:
            grad_lo[kx] = grad_in.astype(BF16)
        elif kx < RADIUS + CELLS:
            grad_mid[kx - RADIUS] = grad_in
        else:
            grad_hi[kx - RADIUS - CELLS] = grad_in.astype(BF16)

    def diagonal(full):
        return jnp.concatenate(
            [full[h * HD : (h + 1) * HD, h * QUERIES : (h + 1) * QUERIES] for h in range(H)], axis=0
        )

    attended = diagonal(mm(vs[...], pbs[...], TN)).astype(BF16)
    dw_out = mm(attended, cot2).astype(BF16)
    grad_query = (diagonal(mm(ks[...], dss[...], TN)) * HD ** (-0.5)).T.astype(BF16)
    grad_in_query = mm(grad_query, wqkv[:, :C], NT).reshape(CELLS, CELLS, Z, C)
    grad_mid[:, RADIUS : RADIUS + CELLS, RADIUS : RADIUS + Z, :] += grad_in_query
    dw_q = mm(inner, grad_query, TN).astype(BF16)
    dw_kv = mm(xs[...].reshape(KEYS, C), gkvs[...], TN).astype(BF16)
    parts = (dw_q, dw_kv, dw_out)
    slot = 0
    for part in parts:
        for start in range(0, part.shape[1], 128):
            dw[slot] = part[:, start : start + 128]
            slot += 1


def local_grads(own, ylo, yhi, xlo, xhi, cot, wqkv, wout):
    whole = pl.BlockSpec(memory_space=pltpu.VMEM)
    return pl.pallas_call(
        local_kernel,
        out_shape=(
            jax.ShapeDtypeStruct((RADIUS, WIDE, ZP, C), BF16),
            jax.ShapeDtypeStruct((CELLS, WIDE, ZP, C), F32),
            jax.ShapeDtypeStruct((RADIUS, WIDE, ZP, C), BF16),
            jax.ShapeDtypeStruct((8, C, 128), BF16),
        ),
        in_specs=[whole] * 8,
        out_specs=(whole,) * 4,
        scratch_shapes=[
            pltpu.VMEM((WIDE, WIDE, ZP, C), BF16),
            pltpu.VMEM((KEYS, C), BF16),
            pltpu.VMEM((KEYS, C), BF16),
            pltpu.VMEM((LANES, C), BF16),
            pltpu.VMEM((LANES, C), BF16),
            pltpu.VMEM((KEYS, LANES), F32),
            pltpu.VMEM((KEYS, LANES), F32),
            pltpu.VMEM((KEYS, LANES), BF16),
            pltpu.VMEM((KEYS, LANES), BF16),
            pltpu.VMEM((KEYS, 2 * C), BF16),
        ],
        compiler_params=pltpu.CompilerParams(vmem_limit_bytes=40 * 1024 * 1024),
    )(own, ylo, yhi, xlo, xhi, cot, wqkv, wout)


def shifted(block, axes, distance):
    size = lax.axis_size(axes)
    return lax.ppermute(block, axes, [(i, (i + distance) % size) for i in range(size)])


GX = ("xh", "y", "core")
GY = ("z", "xl")
PLANE = ("xh", "y", "xl")


def summed_weights(dw):
    core = lax.axis_index("core")
    halves = dw.reshape(2, 16, 64, 128)
    mine = lax.dynamic_index_in_dim(halves, core, 0, keepdims=False)
    other = lax.dynamic_index_in_dim(halves, 1 - core, 0, keepdims=False)
    swap = [(0, 1), (1, 0)]
    half = (mine.astype(F32) + lax.ppermute(other, "core", swap).astype(F32)).astype(BF16)
    chunks = lax.all_to_all(half, PLANE, 0, 0)
    chunk = jnp.sum(chunks.astype(F32), axis=0).astype(BF16)
    columns = lax.all_to_all(jnp.broadcast_to(chunk[None], (8, 64, 128)), "z", 0, 0)
    chunk = jnp.sum(columns.astype(F32), axis=0).astype(BF16)
    half = lax.all_to_all(jnp.broadcast_to(chunk[None], (16, 64, 128)), PLANE, 0, 0)
    other = lax.ppermute(half, "core", swap)
    low = jnp.where(core == 0, half, other).reshape(4, C, 128)
    high = jnp.where(core == 0, other, half).reshape(4, C, 128)
    whole = jnp.concatenate([low, high], axis=0).astype(F32)
    wide = whole.transpose(1, 0, 2).reshape(C, 4 * C)
    return wide[:, : 3 * C], wide[:, 3 * C :]


def body(inputs, cotangent, w_qkv, w_out):
    ylo = shifted(inputs[:, CELLS - RADIUS :], GY, 1)
    yhi = shifted(inputs[:, :RADIUS], GY, -1)
    wide = jnp.concatenate([ylo, inputs, yhi], axis=1)
    xlo = shifted(wide[CELLS - RADIUS :], GX, 1)
    xhi = shifted(wide[:RADIUS], GX, -1)
    grad_lo, grad_mid, grad_hi, dw = local_grads(
        inputs, ylo, yhi, xlo, xhi, cotangent, w_qkv, w_out
    )
    from_next = shifted(grad_lo, GX, -1).astype(F32)
    from_before = shifted(grad_hi, GX, 1).astype(F32)
    rest = ((0, 0), (0, 0), (0, 0))
    grad_mid = (
        grad_mid
        + jnp.pad(from_next, ((CELLS - RADIUS, 0),) + rest)
        + jnp.pad(from_before, ((0, CELLS - RADIUS),) + rest)
    )
    middle = grad_mid[:, RADIUS : RADIUS + CELLS]
    from_next = shifted(grad_mid[:, :RADIUS].astype(BF16), GY, -1).astype(F32)
    from_before = shifted(grad_mid[:, RADIUS + CELLS :].astype(BF16), GY, 1).astype(F32)
    rest = ((0, 0), (0, 0))
    grad_inputs = (
        middle
        + jnp.pad(from_next, ((0, 0), (CELLS - RADIUS, 0)) + rest)
        + jnp.pad(from_before, ((0, 0), (0, CELLS - RADIUS)) + rest)
    )
    grad_inputs = grad_inputs[:, :, :ZE].astype(BF16)
    grad_wqkv, grad_wout = summed_weights(dw)
    return grad_inputs, grad_wqkv, grad_wout


def solution(mesh):
    fine = Mesh(mesh.devices.reshape(2, 4, 2, 8, 2), ("xh", "y", "core", "z", "xl"))
    split = P(GX, GY, None, None)
    return jax.shard_map(
        body,
        mesh=fine,
        in_specs=(split, split, P(), P()),
        out_specs=(split, P(), P()),
        check_vma=False,
    )
```

time: 598 us -> 82.7 us (0.14)
  waiting for transfers between devices: 283 us -> 27.8 us
  local copies, waits for them, and re-layouts: 172 us -> 5.61 us
  loops' own time: 42.1 us -> 0 us
  matrix products: 34.4 us -> 0 us
  other arithmetic: 29.6 us -> 1.14 us
  starting transfers between devices: 19.2 us -> 39.6 us
  between operations: 14.4 us -> 0.85 us
  Pallas kernels: 0 us -> 7.15 us
    psum x1 -> x0, waiting for transfers between devices: 259 us -> none  [body(): totals = lax.psum((grad_wqkv_part, grad_wout_part), ('gx', 'gy'))]
    dynamic_update_slice x7 -> x0, local copies, waits for them, and re-layouts: 63.4 us -> none  [key_pass(): lax.dynamic_update_slice_in_dim(grad_grown, current + frame, step_x, 0)]
    dynamic_slice x42 -> x0, local copies, waits for them, and re-layouts: 55 us -> none  [the longest x21 42.7 us: slab_at(): lax.dynamic_slice_in_dim(keyval, step_x, rows_x, 0)]
    another operation x3 -> x0, loops' own time: 42.1 us -> none  [the longest x1 14.2 us: body(): finals = lax.scan(key_pass, initial, steps_x)[0]]
    dot_general x69 -> x0, matrix products: 34.4 us -> none  [the longest x7 12.6 us: key_pass(): jnp.einsum('xhqk,xkhd->xqhd', grad_scores, keys_all, preferred_element_ty...]
    add x21 -> x0, other arithmetic: 20.8 us -> none  [the longest x7 20.6 us: key_pass(): current + frame]
    all_to_all x0 -> x3, waiting for transfers between devices: none -> 20 us  [the longest x1 7.78 us: summed_weights(): lax.all_to_all(jnp.broadcast_to(chunk[None], (8, 64, 128)), 'z', 0, 0)]
    ppermute x8 -> x10, waiting for transfers between devices: 23.8 us -> 7.77 us  [the longest x8 6.24 us: shifted(): lax.ppermute(block, axes, [(i, (i + distance) % size) for i in range(size)])]
  transfers between devices with their start and end apart: 9 -> 13, of which waited for: 9 -> 7; matrix products, arithmetic and copies ran while one was open for 2% -> 2% of each run, Pallas kernels for 0% -> 0%
where the time goes in v1:
time: 82.7 us; the launch traced here: 82.2 us
  starting transfers between devices  39.6 us (48%)
  waiting for transfers between devices  27.8 us (34%)
  Pallas kernels  7.15 us (9%)
  local copies, waits for them, and re-layouts  5.61 us (7%)
  other arithmetic  1.14 us (1%)
  between operations  0.85 us (1%)
    ppermute x8, starting transfers between devices, shifted(): lax.ppermute(block, axes, [(i, (i + distance) % size) for i in range(size)])  13.5 us
    ppermute x1, starting transfers between devices, summed_weights(): lax.ppermute(other, 'core', swap).astype(F32)  8.31 us
    all_to_all x1, waiting for transfers between devices, summed_weights(): lax.all_to_all(jnp.broadcast_to(chunk[None], (8, 64, 128)), 'z', 0, 0)  7.78 us
    pallas_call x1, Pallas kernels, local_grads(): pl.pallas_call(local_kernel, out_shape=(jax.ShapeDtypeStruct((RADIUS, WID...  7.15 us
    all_to_all x1, starting transfers between devices, summed_weights(): lax.all_to_all(jnp.broadcast_to(chunk[None], (8, 64, 128)), 'z', 0, 0)  6.64 us
    ppermute x8, waiting for transfers between devices, shifted(): lax.ppermute(block, axes, [(i, (i + distance) % size) for i in range(size)])  6.24 us
    all_to_all x1, waiting for transfers between devices, summed_weights(): chunks = lax.all_to_all(half, PLANE, 0, 0)  6.23 us
    all_to_all x1, waiting for transfers between devices, summed_weights(): lax.all_to_all(jnp.broadcast_to(chunk[None], (16, 64, 128)), PLANE, 0, 0)  6.04 us
  transfers between devices with their start and end apart: 13, of which 7 were waited for; matrix products, arithmetic and copies ran while one was open for 2% of the time, Pallas kernels for 0%

profile of v1, /device:TPU:1, one launch (start us, length us, event | category | flops | bytes accessed | tf_op | source)
XLA Modules:
  0.0 82.2 jit_solution(6670245671867079226)
XLA Ops:
  0.6 0.9 %copy.28.own = bf16[4,4,14,256]{3,2,1,0:T(8,128)(2,1)S(1)} copy(bf16[4,4,14,256]{3,1,2,0:T(4,128)(2,1)} %param.4) | data formatting | bytes 229376 | tf_op args[0]
  1.6 0.0 copy-start.3
  1.6 2.1 %collective-permute-start = (bf16[4,3,14,256]{3,2,1,0:T(8,128)(2,1)S(1)}, bf16[4,3,14,256]{3,2,1,0:T(8,128)(2,1)S(1)}, u32[]{:S(2)}, u32[]{:S(2)}) collective-permute-start(bf16[4,3,14,256]{3,2,1,0:T(8,128)(2,1)S(1)} %get-tuple-element.32), channel_id=1, source_target_pairs={{0,1},{1,2},{2,3},{3,4},{4,5},{5,6},{6,7},{7,8},{8,9},{9,10},{10,1... | collective-permute-start | bytes 258056 | tf_op jit(solution)/shard_map/ppermute | solution.py:155
  3.7 5.4 %collective-permute-start.1 = (bf16[4,3,14,256]{3,2,1,0:T(8,128)(2,1)S(1)}, bf16[4,3,14,256]{3,2,1,0:T(8,128)(2,1)S(1)}, u32[]{:S(2)}, u32[]{:S(2)}) collective-permute-start(bf16[4,3,14,256]{3,2,1,0:T(8,128)(2,1)S(1)} %get-tuple-element.31), channel_id=1, source_target_pairs={{0,15},{1,0},{2,1},{3,2},{4,3},{5,4},{6,5},{7,6},{8,7},{9,8},{10,9... | collective-permute-start | bytes 258056 | tf_op jit(solution)/shard_map/ppermute | solution.py:155
  9.1 2.4 %collective-permute-done.ylo = bf16[4,3,14,256]{3,2,1,0:T(8,128)(2,1)S(1)} collective-permute-done((bf16[4,3,14,256]{3,2,1,0:T(8,128)(2,1)S(1)}, bf16[4,3,14,256]{3,2,1,0:T(8,128)(2,1)S(1)}, u32[]{:S(2)}, u32[]{:S(2)}) %collective-permute-start) | collective-permute-done | bytes 86048 | tf_op jit(solution)/shard_map/ppermute | solution.py:155
  11.5 0.0 copy-done.3
  11.6 0.0 collective-permute-done.1.yhi
  11.6 0.0 copy-start
  11.6 0.0 copy-start.1
  11.6 0.0 copy-start.2
  11.7 1.3 %collective-permute-start.3 = (bf16[3,10,14,256]{3,2,1,0:T(8,128)(2,1)S(1)}, bf16[3,10,14,256]{3,2,1,0:T(8,128)(2,1)S(1)}, u32[]{:S(2)}, u32[]{:S(2)}) collective-permute-start(bf16[3,10,14,256]{3,2,1,0:T(8,128)(2,1)S(1)} %get-tuple-element.29), channel_id=1, source_target_pairs={{0,240},{16,0},{32,16},{48,32},{64,48},{80,64},{96,80},{112,96},{1... | collective-permute-start | bytes 645128 | tf_op jit(solution)/shard_map/ppermute | solution.py:155
  13.0 1.3 %collective-permute-start.2 = (bf16[3,10,14,256]{3,2,1,0:T(8,128)(2,1)S(1)}, bf16[3,10,14,256]{3,2,1,0:T(8,128)(2,1)S(1)}, u32[]{:S(2)}, u32[]{:S(2)}) collective-permute-start(bf16[3,10,14,256]{3,2,1,0:T(8,128)(2,1)S(1)} %get-tuple-element.30), channel_id=1, source_target_pairs={{0,16},{16,32},{32,48},{48,64},{64,80},{80,96},{96,112},{112,128},... | collective-permute-start | bytes 645128 | tf_op jit(solution)/shard_map/ppermute | solution.py:155
  14.3 3.8 %collective-permute-done.3.xhi = bf16[3,10,14,256]{3,2,1,0:T(8,128)(2,1)S(1)} collective-permute-done((bf16[3,10,14,256]{3,2,1,0:T(8,128)(2,1)S(1)}, bf16[3,10,14,256]{3,2,1,0:T(8,128)(2,1)S(1)}, u32[]{:S(2)}, u32[]{:S(2)}) %collective-permute-start.3) | collective-permute-done | bytes 215072 | tf_op jit(solution)/shard_map/ppermute | solution.py:155
  18.0 0.0 collective-permute-done.2.xlo
  18.1 0.0 copy-done
  18.1 0.0 copy-done.1
  18.1 0.0 copy-done.2
  18.1 7.2 %shard_map.67 = (bf16[3,10,16,256]{3,2,1,0:T(8,128)(2,1)S(1)}, f32[4,10,16,256]{3,2,1,0:T(8,128)S(1)}, bf16[3,10,16,256]{3,2,1,0:T(8,128)(2,1)S(1)}, bf16[8,256,128]{2,1,0:T(8,128)(2,1)S(1)}) custom-call(bf16[4,4,14,256]{3,2,1,0:T(8,128)(2,1)S(1)} %copy.28.own, bf16[4,3,14,256]{3,2,1,0:T(8,128)(2,1)S(1)} %collective-permute-done.ylo, ...), custom_call_target="tpu_custom_call" | custom-call | tf_op jit(solution)/shard_map/pallas_call | solution.py:127
  25.3 8.3 %collective-permute-start.8 = (bf16[16,64,128]{2,1,0:T(8,128)(2,1)S(1)}, bf16[16,64,128]{2,1,0:T(8,128)(2,1)S(1)}, u32[]{:S(2)}, u32[]{:S(2)}) collective-permute-start(bf16[16,64,128]{2,1,0:T(8,128)(2,1)S(1)} %dynamic-slice_bitcast_fusion), channel_id=1, source_target_pairs={{0,16},{16,0},{1,17},{17,1},{2,18},{18,2},{3,19},{19,3},{4,20},{20... | collective-permute-start | bytes 786440 | tf_op jit(solution)/shard_map/ppermute | solution.py:169
  33.6 1.2 %collective-permute-done.8 = bf16[16,64,128]{2,1,0:T(8,128)(2,1)S(1)} collective-permute-done((bf16[16,64,128]{2,1,0:T(8,128)(2,1)S(1)}, bf16[16,64,128]{2,1,0:T(8,128)(2,1)S(1)}, u32[]{:S(2)}, u32[]{:S(2)}) %collective-permute-start.8) | collective-permute-done | bytes 262176 | tf_op jit(solution)/shard_map/ppermute | solution.py:169
  34.7 0.8 fusion
  35.5 3.5 %all-to-all-start = ((bf16[16,64,128]{2,1,0:T(8,128)(2,1)}), bf16[16,64,128]{2,1,0:T(8,128)(2,1)S(1)}, u32[]{:S(2)}, u32[]{:S(2)}) async-start(bf16[16,64,128]{2,1,0:T(8,128)(2,1)} %fusion), calls=%async_computation | async-start | bytes 524288 | tf_op jit(solution)/shard_map/all_to_all | solution.py:170
  39.1 0.5 collective-permute-start.4
  39.5 1.4 %collective-permute-start.5 = (bf16[3,10,16,256]{3,2,1,0:T(8,128)(2,1)S(1)}, bf16[3,10,16,256]{3,2,1,0:T(8,128)(2,1)S(1)}, u32[]{:S(2)}, u32[]{:S(2)}) collective-permute-start(bf16[3,10,16,256]{3,2,1,0:T(8,128)(2,1)S(1)} %get-tuple-element.9), channel_id=1, source_target_pairs={{0,16},{16,32},{32,48},{48,64},{64,80},{80,96},{96,112},{112,128},... | collective-permute-start | bytes 737288 | tf_op jit(solution)/shard_map/ppermute | solution.py:155
  40.9 6.2 %all-to-all-done = bf16[16,64,128]{2,1,0:T(8,128)(2,1)S(1)} async-done(((bf16[16,64,128]{2,1,0:T(8,128)(2,1)}), bf16[16,64,128]{2,1,0:T(8,128)(2,1)S(1)}, u32[]{:S(2)}, u32[]{:S(2)}) %all-to-all-start) | async-done | bytes 262176 | tf_op jit(solution)/shard_map/all_to_all | solution.py:170
  47.2 0.7 broadcast_in_dim.4
  47.9 6.6 %all-to-all-start.1 = ((bf16[8,64,128]{2,1,0:T(8,128)(2,1)}), bf16[8,64,128]{2,1,0:T(8,128)(2,1)S(1)}, u32[]{:S(2)}, u32[]{:S(2)}) async-start(bf16[8,64,128]{2,1,0:T(8,128)(2,1)} %broadcast_in_dim.4), calls=%async_computation.1 | async-start | bytes 262144 | tf_op jit(solution)/shard_map/all_to_all | solution.py:172
  54.5 0.0 collective-permute-done.4
  54.5 0.0 collective-permute-done.5
  54.5 0.1 fusion.3
  54.7 7.8 %all-to-all-done.1 = bf16[8,64,128]{2,1,0:T(8,128)(2,1)S(1)} async-done(((bf16[8,64,128]{2,1,0:T(8,128)(2,1)}), bf16[8,64,128]{2,1,0:T(8,128)(2,1)S(1)}, u32[]{:S(2)}, u32[]{:S(2)}) %all-to-all-start.1) | async-done | bytes 131104 | tf_op jit(solution)/shard_map/all_to_all | solution.py:172
  62.5 0.8 broadcast_in_dim.5
  63.2 3.5 %all-to-all-start.2 = ((bf16[16,64,128]{2,1,0:T(8,128)(2,1)}), bf16[16,64,128]{2,1,0:T(8,128)(2,1)S(1)}, u32[]{:S(2)}, u32[]{:S(2)}) async-start(bf16[16,64,128]{2,1,0:T(8,128)(2,1)} %broadcast_in_dim.5), calls=%async_computation.2 | async-start | bytes 524288 | tf_op jit(solution)/shard_map/all_to_all | solution.py:174
  66.8 0.8 collective-permute-start.6
  67.6 0.8 collective-permute-start.7
  68.3 6.0 %all-to-all-done.2 = bf16[16,64,128]{2,1,0:T(8,128)(2,1)S(1)} async-done(((bf16[16,64,128]{2,1,0:T(8,128)(2,1)}), bf16[16,64,128]{2,1,0:T(8,128)(2,1)S(1)}, u32[]{:S(2)}, u32[]{:S(2)}) %all-to-all-start.2) | async-done | bytes 262176 | tf_op jit(solution)/shard_map/all_to_all | solution.py:174
  74.4 4.1 %collective-permute-start.9 = (bf16[16,64,128]{2,1,0:T(8,128)(2,1)S(1)}, bf16[16,64,128]{2,1,0:T(8,128)(2,1)S(1)}, u32[]{:S(2)}, u32[]{:S(2)}) collective-permute-start(bf16[16,64,128]{2,1,0:T(8,128)(2,1)S(1)} %all-to-all-done.2), channel_id=1, source_target_pairs={{0,16},{16,0},{1,17},{17,1},{2,18},{18,2},{3,19},{19,3},{4,20},{20... | collective-permute-start | bytes 786440 | tf_op jit(solution)/shard_map/ppermute | solution.py:175
  78.5 0.0 collective-permute-done.6
  78.5 0.0 collective-permute-done.7
  78.6 0.7 copy.30
  79.3 0.4 collective-permute-done.9
  79.7 0.1 convert_bitcast_fusion
  79.8 0.3 copy.29
  80.1 0.1 slice.51
  80.2 1.1 %copy.31 = f32[256,768]{1,0:T(8,128)} copy(f32[256,768]{0,1:T(8,128)S(1)} %slice.51) | data formatting | bytes 1572864
  81.3 0.8 %copy.32 = f32[256,256]{1,0:T(8,128)} copy(f32[256,256]{0,1:T(8,128)S(1)} %slice.52) | data formatting | bytes 524288
  (13 shorter events, 0.3 us)
Async XLA Ops:
  1.6 10.0 %copy-start.3 = (bf16[4,4,14,256]{3,1,2,0:T(4,128)(2,1)S(1)}, bf16[4,4,14,256]{3,1,2,0:T(4,128)(2,1)}, u32[]{:S(2)}) copy-start(bf16[4,4,14,256]{3,1,2,0:T(4,128)(2,1)} %param.4) | copy-start | bytes 344068
  1.6 9.9 %collective-permute-start = (bf16[4,3,14,256]{3,2,1,0:T(8,128)(2,1)S(1)}, bf16[4,3,14,256]{3,2,1,0:T(8,128)(2,1)S(1)}, u32[]{:S(2)}, u32[]{:S(2)}) collective-permute-start(bf16[4,3,14,256]{3,2,1,0:T(8,128)(2,1)S(1)} %get-tuple-element.32), channel_id=1, source_target_pairs={{0,1},{1,2},{2,3},{3,4},{4,5},{5,6},{6,7},{7,8},{8,9},{9,10},{10,1... | collective-permute-start | bytes 258056 | tf_op jit(solution)/shard_map/ppermute | solution.py:155
  3.7 7.9 %collective-permute-start.1 = (bf16[4,3,14,256]{3,2,1,0:T(8,128)(2,1)S(1)}, bf16[4,3,14,256]{3,2,1,0:T(8,128)(2,1)S(1)}, u32[]{:S(2)}, u32[]{:S(2)}) collective-permute-start(bf16[4,3,14,256]{3,2,1,0:T(8,128)(2,1)S(1)} %get-tuple-element.31), channel_id=1, source_target_pairs={{0,15},{1,0},{2,1},{3,2},{4,3},{5,4},{6,5},{7,6},{8,7},{9,8},{10,9... | collective-permute-start | bytes 258056 | tf_op jit(solution)/shard_map/ppermute | solution.py:155
  11.6 6.5 %copy-start = (bf16[256,768]{1,0:T(8,128)(2,1)S(1)}, bf16[256,768]{1,0:T(8,128)(2,1)}, u32[]{:S(2)}) copy-start(bf16[256,768]{1,0:T(8,128)(2,1)} %wqkv.1) | copy-start | bytes 1179652
  11.6 6.5 %copy-start.1 = (bf16[256,256]{1,0:T(8,128)(2,1)S(1)}, bf16[256,256]{1,0:T(8,128)(2,1)}, u32[]{:S(2)}) copy-start(bf16[256,256]{1,0:T(8,128)(2,1)} %wout.1) | copy-start | bytes 393220
  11.6 6.4 %copy-start.2 = (bf16[4,4,8,256]{3,2,1,0:T(8,128)(2,1)S(1)}, bf16[4,4,8,256]{3,2,1,0:T(8,128)(2,1)}, u32[]{:S(2)}) copy-start(bf16[4,4,8,256]{3,2,1,0:T(8,128)(2,1)} %cot.1) | copy-start | bytes 196612
  11.7 6.4 %collective-permute-start.3 = (bf16[3,10,14,256]{3,2,1,0:T(8,128)(2,1)S(1)}, bf16[3,10,14,256]{3,2,1,0:T(8,128)(2,1)S(1)}, u32[]{:S(2)}, u32[]{:S(2)}) collective-permute-start(bf16[3,10,14,256]{3,2,1,0:T(8,128)(2,1)S(1)} %get-tuple-element.29), channel_id=1, source_target_pairs={{0,240},{16,0},{32,16},{48,32},{64,48},{80,64},{96,80},{112,96},{1... | collective-permute-start | bytes 645128 | tf_op jit(solution)/shard_map/ppermute | solution.py:155
  13.0 5.1 %collective-permute-start.2 = (bf16[3,10,14,256]{3,2,1,0:T(8,128)(2,1)S(1)}, bf16[3,10,14,256]{3,2,1,0:T(8,128)(2,1)S(1)}, u32[]{:S(2)}, u32[]{:S(2)}) collective-permute-start(bf16[3,10,14,256]{3,2,1,0:T(8,128)(2,1)S(1)} %get-tuple-element.30), channel_id=1, source_target_pairs={{0,16},{16,32},{32,48},{48,64},{64,80},{80,96},{96,112},{112,128},... | collective-permute-start | bytes 645128 | tf_op jit(solution)/shard_map/ppermute | solution.py:155
  25.3 9.5 %collective-permute-start.8 = (bf16[16,64,128]{2,1,0:T(8,128)(2,1)S(1)}, bf16[16,64,128]{2,1,0:T(8,128)(2,1)S(1)}, u32[]{:S(2)}, u32[]{:S(2)}) collective-permute-start(bf16[16,64,128]{2,1,0:T(8,128)(2,1)S(1)} %dynamic-slice_bitcast_fusion), channel_id=1, source_target_pairs={{0,16},{16,0},{1,17},{17,1},{2,18},{18,2},{3,19},{19,3},{4,20},{20... | collective-permute-start | bytes 786440 | tf_op jit(solution)/shard_map/ppermute | solution.py:169
  35.5 11.6 %all-to-all-start = ((bf16[16,64,128]{2,1,0:T(8,128)(2,1)}), bf16[16,64,128]{2,1,0:T(8,128)(2,1)S(1)}, u32[]{:S(2)}, u32[]{:S(2)}) async-start(bf16[16,64,128]{2,1,0:T(8,128)(2,1)} %fusion), calls=%async_computation | async-start | bytes 524288 | tf_op jit(solution)/shard_map/all_to_all | solution.py:170
  39.1 15.5 %collective-permute-start.4 = (bf16[3,10,16,256]{3,2,1,0:T(8,128)(2,1)S(1)}, bf16[3,10,16,256]{3,2,1,0:T(8,128)(2,1)S(1)}, u32[]{:S(2)}, u32[]{:S(2)}) collective-permute-start(bf16[3,10,16,256]{3,2,1,0:T(8,128)(2,1)S(1)} %get-tuple-element.8), channel_id=1, source_target_pairs={{0,240},{16,0},{32,16},{48,32},{64,48},{80,64},{96,80},{112,96},{1... | collective-permute-start | bytes 737288 | tf_op jit(solution)/shard_map/ppermute | solution.py:155
  39.5 15.0 %collective-permute-start.5 = (bf16[3,10,16,256]{3,2,1,0:T(8,128)(2,1)S(1)}, bf16[3,10,16,256]{3,2,1,0:T(8,128)(2,1)S(1)}, u32[]{:S(2)}, u32[]{:S(2)}) collective-permute-start(bf16[3,10,16,256]{3,2,1,0:T(8,128)(2,1)S(1)} %get-tuple-element.9), channel_id=1, source_target_pairs={{0,16},{16,32},{32,48},{48,64},{64,80},{80,96},{96,112},{112,128},... | collective-permute-start | bytes 737288 | tf_op jit(solution)/shard_map/ppermute | solution.py:155
  47.9 14.6 %all-to-all-start.1 = ((bf16[8,64,128]{2,1,0:T(8,128)(2,1)}), bf16[8,64,128]{2,1,0:T(8,128)(2,1)S(1)}, u32[]{:S(2)}, u32[]{:S(2)}) async-start(bf16[8,64,128]{2,1,0:T(8,128)(2,1)} %broadcast_in_dim.4), calls=%async_computation.1 | async-start | bytes 262144 | tf_op jit(solution)/shard_map/all_to_all | solution.py:172
  63.2 11.1 %all-to-all-start.2 = ((bf16[16,64,128]{2,1,0:T(8,128)(2,1)}), bf16[16,64,128]{2,1,0:T(8,128)(2,1)S(1)}, u32[]{:S(2)}, u32[]{:S(2)}) async-start(bf16[16,64,128]{2,1,0:T(8,128)(2,1)} %broadcast_in_dim.5), calls=%async_computation.2 | async-start | bytes 524288 | tf_op jit(solution)/shard_map/all_to_all | solution.py:174
  66.8 11.7 %collective-permute-start.6 = (bf16[4,3,16,256]{3,2,1,0:T(8,128)(2,1)S(1)}, bf16[4,3,16,256]{3,2,1,0:T(8,128)(2,1)S(1)}, u32[]{:S(2)}, u32[]{:S(2)}) collective-permute-start(bf16[4,3,16,256]{3,2,1,0:T(8,128)(2,1)S(1)} %get-tuple-element.27), channel_id=1, source_target_pairs={{0,15},{1,0},{2,1},{3,2},{4,3},{5,4},{6,5},{7,6},{8,7},{9,8},{10,9... | collective-permute-start | bytes 294920 | tf_op jit(solution)/shard_map/ppermute | solution.py:155
  67.6 10.9 %collective-permute-start.7 = (bf16[4,3,16,256]{3,2,1,0:T(8,128)(2,1)S(1)}, bf16[4,3,16,256]{3,2,1,0:T(8,128)(2,1)S(1)}, u32[]{:S(2)}, u32[]{:S(2)}) collective-permute-start(bf16[4,3,16,256]{3,2,1,0:T(8,128)(2,1)S(1)} %get-tuple-element.28), channel_id=1, source_target_pairs={{0,1},{1,2},{2,3},{3,4},{4,5},{5,6},{6,7},{7,8},{8,9},{9,10},{10,1... | collective-permute-start | bytes 294920 | tf_op jit(solution)/shard_map/ppermute | solution.py:155
  74.4 5.3 %collective-permute-start.9 = (bf16[16,64,128]{2,1,0:T(8,128)(2,1)S(1)}, bf16[16,64,128]{2,1,0:T(8,128)(2,1)S(1)}, u32[]{:S(2)}, u32[]{:S(2)}) collective-permute-start(bf16[16,64,128]{2,1,0:T(8,128)(2,1)S(1)} %all-to-all-done.2), channel_id=1, source_target_pairs={{0,16},{16,0},{1,17},{17,1},{2,18},{18,2},{3,19},{19,3},{4,20},{20... | collective-permute-start | bytes 786440 | tf_op jit(solution)/shard_map/ppermute | solution.py:175

commit v2 on v1

--- a/solution.py
+++ b/solution.py
@@ -63,62 +63,55 @@
     far_z = outside(lax.broadcasted_iota(jnp.int32, (ZP, QUERIES), 0) - query_z)
     far_yz = [far_z + outside(ky - query_y) for ky in range(WIDE)]
 
-    total = jnp.zeros((8, LANES), F32)
-    weighted = jnp.zeros((8, LANES), F32)
-    for kx in range(WIDE):
-        rows = slice(kx * ROWS, (kx + 1) * ROWS)
-        kv = mm(xs[kx].reshape(ROWS, C), wqkv[:, C:]).astype(BF16)
-        ks[rows, :] = kv[:, :C]
-        vs[rows, :] = kv[:, C:]
-        far_x = outside(kx - query_x)
-        far = jnp.concatenate([part + far_x for part in far_yz], axis=0)
-        scores = mm(kv[:, :C], qbd[...], NT) + jnp.concatenate([far] * H, axis=1)
-        exps = jnp.exp(scores)
-        grad_probs = mm(kv[:, C:], gabd[...], NT)
-        es[rows, :] = exps
-        gps[rows, :] = grad_probs
-        total += jnp.sum(exps.reshape(ROWS // 8, 8, LANES), axis=0)
-        weighted += jnp.sum((exps * grad_probs).reshape(ROWS // 8, 8, LANES), axis=0)
-
-    inverse = 1.0 / jnp.sum(total, axis=0, keepdims=True)
-    balance = jnp.sum(weighted, axis=0, keepdims=True) * inverse
-
-    for kx in range(WIDE):
-        rows = slice(kx * ROWS, (kx + 1) * ROWS)
-        probs = es[rows, :] * inverse
-        prob_bf = probs.astype(BF16)
-        slopes = (probs * (gps[rows, :] - balance)).astype(BF16)
-        pbs[rows, :] = prob_bf
-        dss[rows, :] = slopes
-        grad_kv = jnp.concatenate(
-            [mm(slopes, qbd[...]).astype(BF16), mm(prob_bf, gabd[...]).astype(BF16)], axis=1
-        )
-        gkvs[rows, :] = grad_kv
-        grad_in = mm(grad_kv, wqkv[:, C:], NT).reshape(WIDE, ZP, C)
-        if kx < RADIUS:
-            grad_lo[kx] = grad_in.astype(BF16)
-        elif kx < RADIUS + CELLS:
-            grad_mid[kx - RADIUS] = grad_in
-        else:
-            grad_hi[kx - RADIUS - CELLS] = grad_in.astype(BF16)
-
-    def diagonal(full):
-        return jnp.concatenate(
-            [full[h * HD : (h + 1) * HD, h * QUERIES : (h + 1) * QUERIES] for h in range(H)], axis=0
-        )
-
-    attended = diagonal(mm(vs[...], pbs[...], TN)).astype(BF16)
+    kv = mm(xs[...].reshape(KEYS, C), wqkv[:, C:]).astype(BF16)
+    ks[...] = kv[:, :C]
+    vs[...] = kv[:, C:]
+    scores = mm(kv[:, :C], qbd[...], NT)
+    grad_probs = mm(kv[:, C:], gabd[...], NT)
+    far = jnp.concatenate([part + outside(kx - query_x) for kx in range(WIDE) for part in far_yz], axis=0)
+    exps = jnp.exp(scores + jnp.concatenate([far] * H, axis=1))
+    es[...] = exps
+    gps[...] = grad_probs
+    inverse = 1.0 / jnp.sum(exps, axis=0, keepdims=True)
+    balance = jnp.sum(exps * grad_probs, axis=0, keepdims=True) * inverse
+
+    probs = es[...] * inverse
+    prob_bf = probs.astype(BF16)
+    slopes = (probs * (gps[...] - balance)).astype(BF16)
+    pbs[...] = prob_bf
+    dss[...] = slopes
+    grad_kv = jnp.concatenate(
+        [mm(slopes, qbd[...]).astype(BF16), mm(prob_bf, gabd[...]).astype(BF16)], axis=1
+    )
+    gkvs[...] = grad_kv
+    grad_in = mm(grad_kv, wqkv[:, C:], NT).reshape(WIDE, WIDE, ZP, C)
+    grad_lo[...] = grad_in[:RADIUS].astype(BF16)
+    grad_mid[...] = grad_in[RADIUS : RADIUS + CELLS]
+    grad_hi[...] = grad_in[RADIUS + CELLS :].astype(BF16)
+
+    def over_keys(values, weights):
+        out = []
+        for pair in range(H // 2):
+            full = mm(
+                values[:, pair * 2 * HD : (pair + 1) * 2 * HD],
+                weights[:, pair * 2 * QUERIES : (pair + 1) * 2 * QUERIES],
+                TN,
+            )
+            out += [full[:HD, :QUERIES], full[HD:, QUERIES:]]
+        return jnp.concatenate(out, axis=0)
+
+    attended = over_keys(vs, pbs).astype(BF16)
     dw_out = mm(attended, cot2).astype(BF16)
-    grad_query = (diagonal(mm(ks[...], dss[...], TN)) * HD ** (-0.5)).T.astype(BF16)
+    grad_query = (over_keys(ks, dss) * HD ** (-0.5)).T.astype(BF16)
     grad_in_query = mm(grad_query, wqkv[:, :C], NT).reshape(CELLS, CELLS, Z, C)
     grad_mid[:, RADIUS : RADIUS + CELLS, RADIUS : RADIUS + Z, :] += grad_in_query
     dw_q = mm(inner, grad_query, TN).astype(BF16)
     dw_kv = mm(xs[...].reshape(KEYS, C), gkvs[...], TN).astype(BF16)
-    parts = (dw_q, dw_kv, dw_out)
     slot = 0
-    for part in parts:
+    for part in (dw_q, dw_kv, dw_out):
         for start in range(0, part.shape[1], 128):
-            dw[slot] = part[:, start : start + 128]
+            for half in range(2):
+                dw[half, slot] = part[half * 128 : (half + 1) * 128, start : start + 128]
             slot += 1
 
 
@@ -130,7 +123,7 @@
             jax.ShapeDtypeStruct((RADIUS, WIDE, ZP, C), BF16),
             jax.ShapeDtypeStruct((CELLS, WIDE, ZP, C), F32),
             jax.ShapeDtypeStruct((RADIUS, WIDE, ZP, C), BF16),
-            jax.ShapeDtypeStruct((8, C, 128), BF16),
+            jax.ShapeDtypeStruct((2, 8, 128, 128), BF16),
         ),
         in_specs=[whole] * 8,
         out_specs=(whole,) * 4,
@@ -150,9 +143,49 @@
     )(own, ylo, yhi, xlo, xhi, cot, wqkv, wout)
 
 
-def shifted(block, axes, distance):
+def neighbours(easy, hard, axes):
     size = lax.axis_size(axes)
-    return lax.ppermute(block, axes, [(i, (i + distance) % size) for i in range(size)])
+    near = [(i, i ^ 1) for i in range(size)]
+    far = [(i, (i + 1 if i % 2 else i - 1) % size) for i in range(size)]
+    from_far = lax.ppermute(hard, axes, far)
+    return lax.ppermute(easy, axes, near), from_far
+
+
+def exchanged(low, high, axes):
+    first = lax.axis_index(axes) % 2 == 0
+    near, far = neighbours(jnp.where(first, high, low), jnp.where(first, low, high), axes)
+    return jnp.where(first, far, near), jnp.where(first, near, far)
+
+
+def rims(block, dim, axes):
+    odd = lax.axis_index(axes) % 2
+    easy = lax.dynamic_slice_in_dim(block, 1 - odd, RADIUS, dim)
+    hard = lax.dynamic_slice_in_dim(block, odd, RADIUS, dim)
+    near, far = neighbours(easy, hard, axes)
+    return jnp.where(odd == 0, far, near), jnp.where(odd == 0, near, far)
+
+
+def place_kernel(half, other, wqkv, wout):
+    core = lax.axis_index("core")
+    for part, place in ((half, core), (other, 1 - core)):
+        rows = pl.ds(pl.multiple_of(place * 128, 128), 128)
+        for slot in range(8):
+            tile = part[slot].astype(F32)
+            if slot < 6:
+                wqkv[rows, slot * 128 : (slot + 1) * 128] = tile
+            else:
+                wout[rows, (slot - 6) * 128 : (slot - 5) * 128] = tile
+
+
+def placed(half, other):
+    whole = pl.BlockSpec(memory_space=pltpu.VMEM)
+    return pl.pallas_call(
+        place_kernel,
+        out_shape=(jax.ShapeDtypeStruct((C, 3 * C), F32), jax.ShapeDtypeStruct((C, C), F32)),
+        in_specs=[whole] * 2,
+        out_specs=(whole,) * 2,
+        compiler_params=pltpu.CompilerParams(vmem_limit_bytes=8 * 1024 * 1024),
+    )(half.reshape(8, 128, 128), other.reshape(8, 128, 128))
 
 
 GX = ("xh", "y", "core")
@@ -173,24 +206,18 @@
     chunk = jnp.sum(columns.astype(F32), axis=0).astype(BF16)
     half = lax.all_to_all(jnp.broadcast_to(chunk[None], (16, 64, 128)), PLANE, 0, 0)
     other = lax.ppermute(half, "core", swap)
-    low = jnp.where(core == 0, half, other).reshape(4, C, 128)
-    high = jnp.where(core == 0, other, half).reshape(4, C, 128)
-    whole = jnp.concatenate([low, high], axis=0).astype(F32)
-    wide = whole.transpose(1, 0, 2).reshape(C, 4 * C)
-    return wide[:, : 3 * C], wide[:, 3 * C :]
+    return placed(half, other)
 
 
 def body(inputs, cotangent, w_qkv, w_out):
-    ylo = shifted(inputs[:, CELLS - RADIUS :], GY, 1)
-    yhi = shifted(inputs[:, :RADIUS], GY, -1)
+    ylo, yhi = rims(inputs, 1, GY)
     wide = jnp.concatenate([ylo, inputs, yhi], axis=1)
-    xlo = shifted(wide[CELLS - RADIUS :], GX, 1)
-    xhi = shifted(wide[:RADIUS], GX, -1)
+    xlo, xhi = rims(wide, 0, GX)
     grad_lo, grad_mid, grad_hi, dw = local_grads(
         inputs, ylo, yhi, xlo, xhi, cotangent, w_qkv, w_out
     )
-    from_next = shifted(grad_lo, GX, -1).astype(F32)
-    from_before = shifted(grad_hi, GX, 1).astype(F32)
+    from_before, from_next = exchanged(grad_lo, grad_hi, GX)
+    from_before, from_next = from_before.astype(F32), from_next.astype(F32)
     rest = ((0, 0), (0, 0), (0, 0))
     grad_mid = (
         grad_mid
@@ -198,8 +225,10 @@
         + jnp.pad(from_before, ((0, CELLS - RADIUS),) + rest)
     )
     middle = grad_mid[:, RADIUS : RADIUS + CELLS]
-    from_next = shifted(grad_mid[:, :RADIUS].astype(BF16), GY, -1).astype(F32)
-    from_before = shifted(grad_mid[:, RADIUS + CELLS :].astype(BF16), GY, 1).astype(F32)
+    low = grad_mid[:, :RADIUS].astype(BF16)
+    high = grad_mid[:, RADIUS + CELLS :].astype(BF16)
+    from_before, from_next = exchanged(low, high, GY)
+    from_before, from_next = from_before.astype(F32), from_next.astype(F32)
     rest = ((0, 0), (0, 0))
     grad_inputs = (
         middle

time: 82.7 us -> 78.6 us (0.950)
  local copies, waits for them, and re-layouts: 5.61 us -> 3.18 us
  starting transfers between devices: 39.6 us -> 38.1 us
  Pallas kernels: 7.15 us -> 5.71 us
  waiting for transfers between devices: 27.8 us -> 29 us
    ppermute x1, starting transfers between devices: 8.31 us -> 3.94 us  [summed_weights(): lax.ppermute(other, 'core', swap).astype(F32)]
    all_to_all x1, starting transfers between devices: 3.53 us -> 6.98 us  [summed_weights(): chunks = lax.all_to_all(half, PLANE, 0, 0)]
    pallas_call x1, Pallas kernels: 7.15 us -> 4.68 us  [local_grads(): pl.pallas_call(local_kernel, out_shape=(jax.ShapeDtypeStruct((RADIUS, WID...]
    unnamed x14 -> x8, local copies, waits for them, and re-layouts: 3.66 us -> 1.64 us
    all_to_all x1, waiting for transfers between devices: 6.23 us -> 7.47 us  [summed_weights(): chunks = lax.all_to_all(half, PLANE, 0, 0)]
    ppermute x8, starting transfers between devices: 13.5 us -> 12.4 us  [the longest x4 6.92 us: neighbours(): from_far = lax.ppermute(hard, axes, far)]
    pallas_call x0 -> x1, Pallas kernels: none -> 1.03 us  [placed(): pl.pallas_call(place_kernel, out_shape=(jax.ShapeDtypeStruct((C, 3 * C),...]
    ppermute x1, starting transfers between devices: 4.1 us -> 5.07 us  [summed_weights(): other = lax.ppermute(half, 'core', swap)]
where the time goes in v2:
time: 78.6 us; the launch traced here: 78.1 us
  starting transfers between devices  38.1 us (48%)
  waiting for transfers between devices  29 us (37%)
  Pallas kernels  5.71 us (7%)
  local copies, waits for them, and re-layouts  3.18 us (4%)
  other arithmetic  1.24 us (2%)
  between operations  0.83 us (1%)
    all_to_all x1, waiting for transfers between devices, summed_weights(): lax.all_to_all(jnp.broadcast_to(chunk[None], (8, 64, 128)), 'z', 0, 0)  7.79 us
    all_to_all x1, waiting for transfers between devices, summed_weights(): chunks = lax.all_to_all(half, PLANE, 0, 0)  7.47 us
    all_to_all x1, starting transfers between devices, summed_weights(): chunks = lax.all_to_all(half, PLANE, 0, 0)  6.98 us
    ppermute x4, starting transfers between devices, neighbours(): from_far = lax.ppermute(hard, axes, far)  6.92 us
    ppermute x4, waiting for transfers between devices, neighbours(): from_far = lax.ppermute(hard, axes, far)  6.33 us
    all_to_all x1, starting transfers between devices, summed_weights(): lax.all_to_all(jnp.broadcast_to(chunk[None], (8, 64, 128)), 'z', 0, 0)  6.21 us
    all_to_all x1, waiting for transfers between devices, summed_weights(): lax.all_to_all(jnp.broadcast_to(chunk[None], (16, 64, 128)), PLANE, 0, 0)  6.12 us
    ppermute x4, starting transfers between devices, neighbours(): return (lax.ppermute(easy, axes, near), from_far)  5.47 us
  transfers between devices with their start and end apart: 13, of which 7 were waited for; matrix products, arithmetic and copies ran while one was open for 2% of the time, Pallas kernels for 0%

profile of v2, /device:TPU:1, one launch (start us, length us, event | category | flops | bytes accessed | tf_op | source)
XLA Modules:
  0.0 78.1 jit_solution(18378349540048844760)
XLA Ops:
  0.6 0.9 %copy.15.own = bf16[4,4,14,256]{3,2,1,0:T(8,128)(2,1)S(1)} copy(bf16[4,4,14,256]{3,1,2,0:T(4,128)(2,1)} %param.4) | data formatting | bytes 229376 | tf_op args[0]
  1.6 2.1 %collective-permute-start.1 = (bf16[4,3,14,256]{3,2,1,0:T(8,128)(2,1)S(1)}, bf16[4,3,14,256]{3,2,1,0:T(8,128)(2,1)S(1)}, u32[]{:S(2)}, u32[]{:S(2)}) collective-permute-start(bf16[4,3,14,256]{3,2,1,0:T(8,128)(2,1)S(1)} %get-tuple-element.37), channel_id=1, source_target_pairs={{0,1},{1,0},{2,3},{3,2},{4,5},{5,4},{6,7},{7,6},{8,9},{9,8},{10,11... | collective-permute-start | bytes 258056 | tf_op jit(solution)/shard_map/ppermute | solution.py:151
  3.7 5.5 %collective-permute-start = (bf16[4,3,14,256]{3,2,1,0:T(8,128)(2,1)S(1)}, bf16[4,3,14,256]{3,2,1,0:T(8,128)(2,1)S(1)}, u32[]{:S(2)}, u32[]{:S(2)}) collective-permute-start(bf16[4,3,14,256]{3,2,1,0:T(8,128)(2,1)S(1)} %get-tuple-element.38), channel_id=1, source_target_pairs={{0,15},{1,2},{2,1},{3,4},{4,3},{5,6},{6,5},{7,8},{8,7},{9,10},{10,... | collective-permute-start | bytes 258056 | tf_op jit(solution)/shard_map/ppermute | solution.py:150
  9.3 0.0 collective-permute-done.1
  9.3 2.0 %collective-permute-done = bf16[4,3,14,256]{3,2,1,0:T(8,128)(2,1)S(1)} collective-permute-done((bf16[4,3,14,256]{3,2,1,0:T(8,128)(2,1)S(1)}, bf16[4,3,14,256]{3,2,1,0:T(8,128)(2,1)S(1)}, u32[]{:S(2)}, u32[]{:S(2)}) %collective-permute-start) | collective-permute-done | bytes 86048 | tf_op jit(solution)/shard_map/ppermute | solution.py:150
  11.3 0.1 pad_maximum_fusion
  11.4 1.9 %collective-permute-start.3 = (bf16[3,10,14,256]{3,2,1,0:T(8,128)(2,1)S(1)}, bf16[3,10,14,256]{3,2,1,0:T(8,128)(2,1)S(1)}, u32[]{:S(2)}, u32[]{:S(2)}) collective-permute-start(bf16[3,10,14,256]{3,2,1,0:T(8,128)(2,1)S(1)} %get-tuple-element.31), channel_id=1, source_target_pairs={{0,16},{16,0},{32,48},{48,32},{64,80},{80,64},{96,112},{112,96},{1... | collective-permute-start | bytes 645128 | tf_op jit(solution)/shard_map/ppermute | solution.py:151
  13.3 1.3 %collective-permute-start.2 = (bf16[3,10,14,256]{3,2,1,0:T(8,128)(2,1)S(1)}, bf16[3,10,14,256]{3,2,1,0:T(8,128)(2,1)S(1)}, u32[]{:S(2)}, u32[]{:S(2)}) collective-permute-start(bf16[3,10,14,256]{3,2,1,0:T(8,128)(2,1)S(1)} %get-tuple-element.32), channel_id=1, source_target_pairs={{0,240},{16,32},{32,16},{48,64},{64,48},{80,96},{96,80},{112,128},... | collective-permute-start | bytes 645128 | tf_op jit(solution)/shard_map/ppermute | solution.py:150
  14.6 0.0 copy-start
  14.6 0.0 copy-start.1
  14.6 0.0 copy-start.2
  14.6 0.0 collective-permute-done.3
  14.6 4.3 %collective-permute-done.2 = bf16[3,10,14,256]{3,2,1,0:T(8,128)(2,1)S(1)} collective-permute-done((bf16[3,10,14,256]{3,2,1,0:T(8,128)(2,1)S(1)}, bf16[3,10,14,256]{3,2,1,0:T(8,128)(2,1)S(1)}, u32[]{:S(2)}, u32[]{:S(2)}) %collective-permute-start.2) | collective-permute-done | bytes 215072 | tf_op jit(solution)/shard_map/ppermute | solution.py:150
  19.0 0.0 copy-done
  19.0 0.0 copy-done.1
  19.0 0.0 copy-done.2
  19.0 4.7 %shard_map.67 = (bf16[3,10,16,256]{3,2,1,0:T(8,128)(2,1)S(1)}, f32[4,10,16,256]{3,2,1,0:T(8,128)S(1)}, bf16[3,10,16,256]{3,2,1,0:T(8,128)(2,1)S(1)}, bf16[2,8,128,128]{3,2,1,0:T(8,128)(2,1)S(1)}) custom-call(bf16[4,4,14,256]{3,2,1,0:T(8,128)(2,1)S(1)} %copy.15.own, bf16[4,3,14,256]{3,2,1,0:T(8,128)(2,1)S(1)} %get-tuple-element.36.ylo, ...), custom_call_target="tpu_custom_call" | custom-call | tf_op jit(solution)/shard_map/pallas_call | solution.py:120
  23.7 3.9 %collective-permute-start.8 = (bf16[16,64,128]{2,1,0:T(8,128)(2,1)S(1)}, bf16[16,64,128]{2,1,0:T(8,128)(2,1)S(1)}, u32[]{:S(2)}, u32[]{:S(2)}) collective-permute-start(bf16[16,64,128]{2,1,0:T(8,128)(2,1)S(1)} %dynamic-slice_bitcast_fusion), channel_id=1, source_target_pairs={{0,16},{16,0},{1,17},{17,1},{2,18},{18,2},{3,19},{19,3},{4,20},{20... | collective-permute-start | bytes 786440 | tf_op jit(solution)/shard_map/ppermute | solution.py:202
  27.7 0.1 collective-permute-start.4
  27.8 0.1 collective-permute-start.5
  27.9 0.9 %collective-permute-done.8 = bf16[16,64,128]{2,1,0:T(8,128)(2,1)S(1)} collective-permute-done((bf16[16,64,128]{2,1,0:T(8,128)(2,1)S(1)}, bf16[16,64,128]{2,1,0:T(8,128)(2,1)S(1)}, u32[]{:S(2)}, u32[]{:S(2)}) %collective-permute-start.8) | collective-permute-done | bytes 262176 | tf_op jit(solution)/shard_map/ppermute | solution.py:202
  28.8 0.8 fusion
  29.6 7.0 %all-to-all-start = ((bf16[16,64,128]{2,1,0:T(8,128)(2,1)}), bf16[16,64,128]{2,1,0:T(8,128)(2,1)S(1)}, u32[]{:S(2)}, u32[]{:S(2)}) async-start(bf16[16,64,128]{2,1,0:T(8,128)(2,1)} %fusion), calls=%async_computation | async-start | bytes 524288 | tf_op jit(solution)/shard_map/all_to_all | solution.py:203
  36.6 0.0 collective-permute-done.4
  36.6 0.0 collective-permute-done.5
  36.7 7.5 %all-to-all-done = bf16[16,64,128]{2,1,0:T(8,128)(2,1)S(1)} async-done(((bf16[16,64,128]{2,1,0:T(8,128)(2,1)}), bf16[16,64,128]{2,1,0:T(8,128)(2,1)S(1)}, u32[]{:S(2)}, u32[]{:S(2)}) %all-to-all-start) | async-done | bytes 262176 | tf_op jit(solution)/shard_map/all_to_all | solution.py:203
  44.2 0.7 broadcast_in_dim.4
  44.9 6.2 %all-to-all-start.1 = ((bf16[8,64,128]{2,1,0:T(8,128)(2,1)}), bf16[8,64,128]{2,1,0:T(8,128)(2,1)S(1)}, u32[]{:S(2)}, u32[]{:S(2)}) async-start(bf16[8,64,128]{2,1,0:T(8,128)(2,1)} %broadcast_in_dim.4), calls=%async_computation.1 | async-start | bytes 262144 | tf_op jit(solution)/shard_map/all_to_all | solution.py:205
  51.1 0.1 fusion.3
  51.2 7.8 %all-to-all-done.1 = bf16[8,64,128]{2,1,0:T(8,128)(2,1)S(1)} async-done(((bf16[8,64,128]{2,1,0:T(8,128)(2,1)}), bf16[8,64,128]{2,1,0:T(8,128)(2,1)S(1)}, u32[]{:S(2)}, u32[]{:S(2)}) %all-to-all-start.1) | async-done | bytes 131104 | tf_op jit(solution)/shard_map/all_to_all | solution.py:205
  59.0 0.8 broadcast_in_dim.5
  59.8 3.5 %all-to-all-start.2 = ((bf16[16,64,128]{2,1,0:T(8,128)(2,1)}), bf16[16,64,128]{2,1,0:T(8,128)(2,1)S(1)}, u32[]{:S(2)}, u32[]{:S(2)}) async-start(bf16[16,64,128]{2,1,0:T(8,128)(2,1)} %broadcast_in_dim.5), calls=%async_computation.2 | async-start | bytes 524288 | tf_op jit(solution)/shard_map/all_to_all | solution.py:207
  63.4 1.3 %collective-permute-start.6 = (bf16[4,3,16,256]{3,2,1,0:T(8,128)(2,1)S(1)}, bf16[4,3,16,256]{3,2,1,0:T(8,128)(2,1)S(1)}, u32[]{:S(2)}, u32[]{:S(2)}) collective-permute-start(bf16[4,3,16,256]{3,2,1,0:T(8,128)(2,1)S(1)} %get-tuple-element.29), channel_id=1, source_target_pairs={{0,1},{1,0},{2,3},{3,2},{4,5},{5,4},{6,7},{7,6},{8,9},{9,8},{10,11... | collective-permute-start | bytes 294920 | tf_op jit(solution)/shard_map/ppermute | solution.py:151
  64.7 0.0 collective-permute-start.7
  64.7 6.1 %all-to-all-done.2 = bf16[16,64,128]{2,1,0:T(8,128)(2,1)S(1)} async-done(((bf16[16,64,128]{2,1,0:T(8,128)(2,1)}), bf16[16,64,128]{2,1,0:T(8,128)(2,1)S(1)}, u32[]{:S(2)}, u32[]{:S(2)}) %all-to-all-start.2) | async-done | bytes 262176 | tf_op jit(solution)/shard_map/all_to_all | solution.py:207
  70.8 5.1 %collective-permute-start.9 = (bf16[16,64,128]{2,1,0:T(8,128)(2,1)S(1)}, bf16[16,64,128]{2,1,0:T(8,128)(2,1)S(1)}, u32[]{:S(2)}, u32[]{:S(2)}) collective-permute-start(bf16[16,64,128]{2,1,0:T(8,128)(2,1)S(1)} %all-to-all-done.2), channel_id=1, source_target_pairs={{0,16},{16,0},{1,17},{17,1},{2,18},{18,2},{3,19},{19,3},{4,20},{20... | collective-permute-start | bytes 786440 | tf_op jit(solution)/shard_map/ppermute | solution.py:208
  75.9 0.0 collective-permute-done.6
  75.9 0.0 collective-permute-done.7
  76.0 0.7 copy.16
  76.7 0.4 collective-permute-done.9
  77.1 1.0 %shard_map.68 = (f32[256,768]{1,0:T(8,128)}, f32[256,256]{1,0:T(8,128)}) custom-call(bf16[8,128,128]{2,1,0:T(8,128)(2,1)S(1)} %bitcast.8, bf16[8,128,128]{2,1,0:T(8,128)(2,1)S(1)} %bitcast.11), custom_call_target="tpu_custom_call" | custom-call | tf_op jit(solution)/shard_map/pallas_call | solution.py:182
  (13 shorter events, 0.4 us)
Async XLA Ops:
  1.6 7.7 %collective-permute-start.1 = (bf16[4,3,14,256]{3,2,1,0:T(8,128)(2,1)S(1)}, bf16[4,3,14,256]{3,2,1,0:T(8,128)(2,1)S(1)}, u32[]{:S(2)}, u32[]{:S(2)}) collective-permute-start(bf16[4,3,14,256]{3,2,1,0:T(8,128)(2,1)S(1)} %get-tuple-element.37), channel_id=1, source_target_pairs={{0,1},{1,0},{2,3},{3,2},{4,5},{5,4},{6,7},{7,6},{8,9},{9,8},{10,11... | collective-permute-start | bytes 258056 | tf_op jit(solution)/shard_map/ppermute | solution.py:151
  3.7 7.6 %collective-permute-start = (bf16[4,3,14,256]{3,2,1,0:T(8,128)(2,1)S(1)}, bf16[4,3,14,256]{3,2,1,0:T(8,128)(2,1)S(1)}, u32[]{:S(2)}, u32[]{:S(2)}) collective-permute-start(bf16[4,3,14,256]{3,2,1,0:T(8,128)(2,1)S(1)} %get-tuple-element.38), channel_id=1, source_target_pairs={{0,15},{1,2},{2,1},{3,4},{4,3},{5,6},{6,5},{7,8},{8,7},{9,10},{10,... | collective-permute-start | bytes 258056 | tf_op jit(solution)/shard_map/ppermute | solution.py:150
  11.4 3.2 %collective-permute-start.3 = (bf16[3,10,14,256]{3,2,1,0:T(8,128)(2,1)S(1)}, bf16[3,10,14,256]{3,2,1,0:T(8,128)(2,1)S(1)}, u32[]{:S(2)}, u32[]{:S(2)}) collective-permute-start(bf16[3,10,14,256]{3,2,1,0:T(8,128)(2,1)S(1)} %get-tuple-element.31), channel_id=1, source_target_pairs={{0,16},{16,0},{32,48},{48,32},{64,80},{80,64},{96,112},{112,96},{1... | collective-permute-start | bytes 645128 | tf_op jit(solution)/shard_map/ppermute | solution.py:151
  13.3 5.6 %collective-permute-start.2 = (bf16[3,10,14,256]{3,2,1,0:T(8,128)(2,1)S(1)}, bf16[3,10,14,256]{3,2,1,0:T(8,128)(2,1)S(1)}, u32[]{:S(2)}, u32[]{:S(2)}) collective-permute-start(bf16[3,10,14,256]{3,2,1,0:T(8,128)(2,1)S(1)} %get-tuple-element.32), channel_id=1, source_target_pairs={{0,240},{16,32},{32,16},{48,64},{64,48},{80,96},{96,80},{112,128},... | collective-permute-start | bytes 645128 | tf_op jit(solution)/shard_map/ppermute | solution.py:150
  14.6 4.4 %copy-start = (bf16[256,768]{1,0:T(8,128)(2,1)S(1)}, bf16[256,768]{1,0:T(8,128)(2,1)}, u32[]{:S(2)}) copy-start(bf16[256,768]{1,0:T(8,128)(2,1)} %wqkv.1) | copy-start | bytes 1179652
  14.6 4.4 %copy-start.1 = (bf16[256,256]{1,0:T(8,128)(2,1)S(1)}, bf16[256,256]{1,0:T(8,128)(2,1)}, u32[]{:S(2)}) copy-start(bf16[256,256]{1,0:T(8,128)(2,1)} %wout.1) | copy-start | bytes 393220
  14.6 4.4 %copy-start.2 = (bf16[4,4,8,256]{3,2,1,0:T(8,128)(2,1)S(1)}, bf16[4,4,8,256]{3,2,1,0:T(8,128)(2,1)}, u32[]{:S(2)}) copy-start(bf16[4,4,8,256]{3,2,1,0:T(8,128)(2,1)} %cot.1) | copy-start | bytes 196612
  23.7 5.1 %collective-permute-start.8 = (bf16[16,64,128]{2,1,0:T(8,128)(2,1)S(1)}, bf16[16,64,128]{2,1,0:T(8,128)(2,1)S(1)}, u32[]{:S(2)}, u32[]{:S(2)}) collective-permute-start(bf16[16,64,128]{2,1,0:T(8,128)(2,1)S(1)} %dynamic-slice_bitcast_fusion), channel_id=1, source_target_pairs={{0,16},{16,0},{1,17},{17,1},{2,18},{18,2},{3,19},{19,3},{4,20},{20... | collective-permute-start | bytes 786440 | tf_op jit(solution)/shard_map/ppermute | solution.py:202
  27.7 8.9 %collective-permute-start.4 = (bf16[3,10,16,256]{3,2,1,0:T(8,128)(2,1)S(1)}, bf16[3,10,16,256]{3,2,1,0:T(8,128)(2,1)S(1)}, u32[]{:S(2)}, u32[]{:S(2)}) collective-permute-start(bf16[3,10,16,256]{3,2,1,0:T(8,128)(2,1)S(1)} %get-tuple-element.25), channel_id=1, source_target_pairs={{0,16},{16,0},{32,48},{48,32},{64,80},{80,64},{96,112},{112,96},{1... | collective-permute-start | bytes 737288 | tf_op jit(solution)/shard_map/ppermute | solution.py:151
  27.8 8.8 %collective-permute-start.5 = (bf16[3,10,16,256]{3,2,1,0:T(8,128)(2,1)S(1)}, bf16[3,10,16,256]{3,2,1,0:T(8,128)(2,1)S(1)}, u32[]{:S(2)}, u32[]{:S(2)}) collective-permute-start(bf16[3,10,16,256]{3,2,1,0:T(8,128)(2,1)S(1)} %get-tuple-element.26), channel_id=1, source_target_pairs={{0,240},{16,32},{32,16},{48,64},{64,48},{80,96},{96,80},{112,128},... | collective-permute-start | bytes 737288 | tf_op jit(solution)/shard_map/ppermute | solution.py:150
  29.6 14.5 %all-to-all-start = ((bf16[16,64,128]{2,1,0:T(8,128)(2,1)}), bf16[16,64,128]{2,1,0:T(8,128)(2,1)S(1)}, u32[]{:S(2)}, u32[]{:S(2)}) async-start(bf16[16,64,128]{2,1,0:T(8,128)(2,1)} %fusion), calls=%async_computation | async-start | bytes 524288 | tf_op jit(solution)/shard_map/all_to_all | solution.py:203
  44.9 14.1 %all-to-all-start.1 = ((bf16[8,64,128]{2,1,0:T(8,128)(2,1)}), bf16[8,64,128]{2,1,0:T(8,128)(2,1)S(1)}, u32[]{:S(2)}, u32[]{:S(2)}) async-start(bf16[8,64,128]{2,1,0:T(8,128)(2,1)} %broadcast_in_dim.4), calls=%async_computation.1 | async-start | bytes 262144 | tf_op jit(solution)/shard_map/all_to_all | solution.py:205
  59.8 11.0 %all-to-all-start.2 = ((bf16[16,64,128]{2,1,0:T(8,128)(2,1)}), bf16[16,64,128]{2,1,0:T(8,128)(2,1)S(1)}, u32[]{:S(2)}, u32[]{:S(2)}) async-start(bf16[16,64,128]{2,1,0:T(8,128)(2,1)} %broadcast_in_dim.5), calls=%async_computation.2 | async-start | bytes 524288 | tf_op jit(solution)/shard_map/all_to_all | solution.py:207
  63.4 12.6 %collective-permute-start.6 = (bf16[4,3,16,256]{3,2,1,0:T(8,128)(2,1)S(1)}, bf16[4,3,16,256]{3,2,1,0:T(8,128)(2,1)S(1)}, u32[]{:S(2)}, u32[]{:S(2)}) collective-permute-start(bf16[4,3,16,256]{3,2,1,0:T(8,128)(2,1)S(1)} %get-tuple-element.29), channel_id=1, source_target_pairs={{0,1},{1,0},{2,3},{3,2},{4,5},{5,4},{6,7},{7,6},{8,9},{9,8},{10,11... | collective-permute-start | bytes 294920 | tf_op jit(solution)/shard_map/ppermute | solution.py:151
  64.7 11.2 %collective-permute-start.7 = (bf16[4,3,16,256]{3,2,1,0:T(8,128)(2,1)S(1)}, bf16[4,3,16,256]{3,2,1,0:T(8,128)(2,1)S(1)}, u32[]{:S(2)}, u32[]{:S(2)}) collective-permute-start(bf16[4,3,16,256]{3,2,1,0:T(8,128)(2,1)S(1)} %get-tuple-element.30), channel_id=1, source_target_pairs={{0,15},{1,2},{2,1},{3,4},{4,3},{5,6},{6,5},{7,8},{8,7},{9,10},{10,... | collective-permute-start | bytes 294920 | tf_op jit(solution)/shard_map/ppermute | solution.py:150
  70.8 6.2 %collective-permute-start.9 = (bf16[16,64,128]{2,1,0:T(8,128)(2,1)S(1)}, bf16[16,64,128]{2,1,0:T(8,128)(2,1)S(1)}, u32[]{:S(2)}, u32[]{:S(2)}) collective-permute-start(bf16[16,64,128]{2,1,0:T(8,128)(2,1)S(1)} %all-to-all-done.2), channel_id=1, source_target_pairs={{0,16},{16,0},{1,17},{17,1},{2,18},{18,2},{3,19},{19,3},{4,20},{20... | collective-permute-start | bytes 786440 | tf_op jit(solution)/shard_map/ppermute | solution.py:208

commit v3 on v2

--- a/solution.py
+++ b/solution.py
@@ -30,18 +30,42 @@
     return lax.dot_general(a, b, dims, preferred_element_type=F32)
 
 
-def local_kernel(
-    own, ylo, yhi, xlo, xhi, cot, wqkv, wout,
-    grad_lo, grad_mid, grad_hi, dw,
-    xs, ks, vs, qbd, gabd, es, gps, pbs, dss, gkvs,
-):
+def far_along(step):
+    return jnp.where((step >= 0) & (step <= 2 * RADIUS), 0.0, FAR)
+
+
+def outside(rows_x):
+    lane = lax.broadcasted_iota(jnp.int32, (1, QUERIES), 1)
+    query_z = lax.broadcasted_iota(jnp.int32, (ZP, QUERIES), 1) % Z
+    far_z = far_along(lax.broadcasted_iota(jnp.int32, (ZP, QUERIES), 0) - query_z)
+    far_yz = [far_z + far_along(ky - lane // Z % CELLS) for ky in range(WIDE)]
+    far_x = [far_along(kx - lane // (CELLS * Z)) for kx in rows_x]
+    far = jnp.concatenate([yz + x for x in far_x for yz in far_yz], axis=0)
+    return jnp.concatenate([far] * H, axis=1)
+
+
+def forward(inputs, rows_x, w_kv, qbd, gabd, ks, vs, es, gps):
+    kv = mm(inputs, w_kv).astype(BF16)
+    ks[...] = kv[:, :C]
+    vs[...] = kv[:, C:]
+    scores = mm(kv[:, :C], qbd, NT)
+    grad_probs = mm(kv[:, C:], gabd, NT)
+    exps = jnp.exp(scores + outside(rows_x))
+    es[...] = exps
+    gps[...] = grad_probs
+    weighted = jnp.sum(exps * grad_probs, axis=0, keepdims=True)
+    return jnp.sum(exps, axis=0, keepdims=True), weighted
+
+
+CENTRE = range(RADIUS, RADIUS + CELLS)
+OUTER = [*range(RADIUS), *range(RADIUS + CELLS, WIDE)]
+
+
+def centre_kernel(own, ylo, yhi, cot, wqkv, wout, xs, qbd, gabd, ks, vs, es, gps, sums):
     xs[...] = jnp.zeros_like(xs)
-    xs[0:RADIUS, :, 0:ZE, :] = xlo[...]
-    xs[RADIUS + CELLS :, :, 0:ZE, :] = xhi[...]
-    xs[RADIUS : RADIUS + CELLS, 0:RADIUS, 0:ZE, :] = ylo[...]
-    xs[RADIUS : RADIUS + CELLS, RADIUS : RADIUS + CELLS, 0:ZE, :] = own[...]
-    xs[RADIUS : RADIUS + CELLS, RADIUS + CELLS :, 0:ZE, :] = yhi[...]
-
+    xs[:, 0:RADIUS, 0:ZE, :] = ylo[...]
+    xs[:, RADIUS : RADIUS + CELLS, 0:ZE, :] = own[...]
+    xs[:, RADIUS + CELLS :, 0:ZE, :] = yhi[...]
     inner = own[...].astype(F32)[:, :, RADIUS : RADIUS + Z, :].reshape(QUERIES, C).astype(BF16)
     cot2 = cot[...].astype(F32).reshape(QUERIES, C).astype(BF16)
     query = mm(inner, wqkv[:, :C]).astype(BF16).astype(F32) * HD ** (-0.5)
@@ -51,96 +75,135 @@
         rows = slice(h * QUERIES, (h + 1) * QUERIES)
         qbd[rows, :] = jnp.where(head == h, query, 0.0).astype(BF16)
         gabd[rows, :] = jnp.where(head == h, grad_attn, 0.0).astype(BF16)
-
-    lane = lax.broadcasted_iota(jnp.int32, (1, QUERIES), 1)
-    query_x = lane // (CELLS * Z)
-    query_y = lane // Z % CELLS
-    query_z = lax.broadcasted_iota(jnp.int32, (ZP, QUERIES), 1) % Z
-
-    def outside(step):
-        return jnp.where((step >= 0) & (step <= 2 * RADIUS), 0.0, FAR)
-
-    far_z = outside(lax.broadcasted_iota(jnp.int32, (ZP, QUERIES), 0) - query_z)
-    far_yz = [far_z + outside(ky - query_y) for ky in range(WIDE)]
-
-    kv = mm(xs[...].reshape(KEYS, C), wqkv[:, C:]).astype(BF16)
-    ks[...] = kv[:, :C]
-    vs[...] = kv[:, C:]
-    scores = mm(kv[:, :C], qbd[...], NT)
-    grad_probs = mm(kv[:, C:], gabd[...], NT)
-    far = jnp.concatenate([part + outside(kx - query_x) for kx in range(WIDE) for part in far_yz], axis=0)
-    exps = jnp.exp(scores + jnp.concatenate([far] * H, axis=1))
-    es[...] = exps
-    gps[...] = grad_probs
-    inverse = 1.0 / jnp.sum(exps, axis=0, keepdims=True)
-    balance = jnp.sum(exps * grad_probs, axis=0, keepdims=True) * inverse
-
-    probs = es[...] * inverse
-    prob_bf = probs.astype(BF16)
-    slopes = (probs * (gps[...] - balance)).astype(BF16)
-    pbs[...] = prob_bf
-    dss[...] = slopes
-    grad_kv = jnp.concatenate(
-        [mm(slopes, qbd[...]).astype(BF16), mm(prob_bf, gabd[...]).astype(BF16)], axis=1
-    )
-    gkvs[...] = grad_kv
-    grad_in = mm(grad_kv, wqkv[:, C:], NT).reshape(WIDE, WIDE, ZP, C)
-    grad_lo[...] = grad_in[:RADIUS].astype(BF16)
-    grad_mid[...] = grad_in[RADIUS : RADIUS + CELLS]
-    grad_hi[...] = grad_in[RADIUS + CELLS :].astype(BF16)
-
-    def over_keys(values, weights):
+    exp_sum, weighted = forward(
+        xs[...].reshape(-1, C), CENTRE, wqkv[:, C:], qbd[...], gabd[...], ks, vs, es, gps
+    )
+    sums[0:1, :] = exp_sum
+    sums[1:2, :] = weighted
+
+
+def main_kernel(
+    own, cot, wqkv, xlo, xhi, xc, qbd, gabd, kc, vc, ec, gpc, sums,
+    gkvc, gkvo, grad_query, dw,
+    xo, ko, vo, eo, gpo, pbc, pbo, dsc, dso,
+):
+    xo[...] = jnp.zeros_like(xo)
+    xo[0:RADIUS, :, 0:ZE, :] = xlo[...]
+    xo[RADIUS:, :, 0:ZE, :] = xhi[...]
+    exp_sum, weighted = forward(
+        xo[...].reshape(-1, C), OUTER, wqkv[:, C:], qbd[...], gabd[...], ko, vo, eo, gpo
+    )
+    inverse = 1.0 / (sums[0:1, :] + exp_sum)
+    balance = (sums[1:2, :] + weighted) * inverse
+    for es, gps, pbs, dss, gkvs in ((ec, gpc, pbc, dsc, gkvc), (eo, gpo, pbo, dso, gkvo)):
+        probs = es[...] * inverse
+        prob_bf = probs.astype(BF16)
+        slopes = (probs * (gps[...] - balance)).astype(BF16)
+        pbs[...] = prob_bf
+        dss[...] = slopes
+        gkvs[:, :C] = mm(slopes, qbd[...]).astype(BF16)
+        gkvs[:, C:] = mm(prob_bf, gabd[...]).astype(BF16)
+
+    def over_keys(parts):
         out = []
         for pair in range(H // 2):
-            full = mm(
-                values[:, pair * 2 * HD : (pair + 1) * 2 * HD],
-                weights[:, pair * 2 * QUERIES : (pair + 1) * 2 * QUERIES],
-                TN,
-            )
+            channels = slice(pair * 2 * HD, (pair + 1) * 2 * HD)
+            lanes = slice(pair * 2 * QUERIES, (pair + 1) * 2 * QUERIES)
+            full = sum(mm(values[:, channels], weights[:, lanes], TN) for values, weights in parts)
             out += [full[:HD, :QUERIES], full[HD:, QUERIES:]]
         return jnp.concatenate(out, axis=0)
 
-    attended = over_keys(vs, pbs).astype(BF16)
+    inner = own[...].astype(F32)[:, :, RADIUS : RADIUS + Z, :].reshape(QUERIES, C).astype(BF16)
+    cot2 = cot[...].astype(F32).reshape(QUERIES, C).astype(BF16)
+    attended = over_keys(((vc, pbc), (vo, pbo))).astype(BF16)
     dw_out = mm(attended, cot2).astype(BF16)
-    grad_query = (over_keys(ks, dss) * HD ** (-0.5)).T.astype(BF16)
-    grad_in_query = mm(grad_query, wqkv[:, :C], NT).reshape(CELLS, CELLS, Z, C)
-    grad_mid[:, RADIUS : RADIUS + CELLS, RADIUS : RADIUS + Z, :] += grad_in_query
-    dw_q = mm(inner, grad_query, TN).astype(BF16)
-    dw_kv = mm(xs[...].reshape(KEYS, C), gkvs[...], TN).astype(BF16)
+    grad_q = (over_keys(((kc, dsc), (ko, dso))) * HD ** (-0.5)).T.astype(BF16)
+    grad_query[...] = grad_q
+    dw_q = mm(inner, grad_q, TN).astype(BF16)
+    dw_kv = mm(xc[...].reshape(-1, C), gkvc[...], TN) + mm(xo[...].reshape(-1, C), gkvo[...], TN)
     slot = 0
-    for part in (dw_q, dw_kv, dw_out):
+    for part in (dw_q, dw_kv.astype(BF16), dw_out):
         for start in range(0, part.shape[1], 128):
             for half in range(2):
                 dw[half, slot] = part[half * 128 : (half + 1) * 128, start : start + 128]
             slot += 1
 
 
-def local_grads(own, ylo, yhi, xlo, xhi, cot, wqkv, wout):
+def inputs_kernel(gkvc, gkvo, grad_query, wqkv, grad_lo, grad_mid, grad_hi):
+    outer = mm(gkvo[...], wqkv[:, C:], NT).astype(BF16).reshape(2 * RADIUS, WIDE, ZP, C)
+    grad_lo[...] = outer[:RADIUS]
+    grad_hi[...] = outer[RADIUS:]
+    grad_mid[...] = mm(gkvc[...], wqkv[:, C:], NT).reshape(CELLS, WIDE, ZP, C)
+    from_query = mm(grad_query[...], wqkv[:, :C], NT).reshape(CELLS, CELLS, Z, C)
+    grad_mid[:, RADIUS : RADIUS + CELLS, RADIUS : RADIUS + Z, :] += from_query
+
+
+def kernel_call(kernel, outs, args, scratch=(), flops=0, mib=24):
     whole = pl.BlockSpec(memory_space=pltpu.VMEM)
     return pl.pallas_call(
-        local_kernel,
-        out_shape=(
-            jax.ShapeDtypeStruct((RADIUS, WIDE, ZP, C), BF16),
-            jax.ShapeDtypeStruct((CELLS, WIDE, ZP, C), F32),
-            jax.ShapeDtypeStruct((RADIUS, WIDE, ZP, C), BF16),
-            jax.ShapeDtypeStruct((2, 8, 128, 128), BF16),
-        ),
-        in_specs=[whole] * 8,
-        out_specs=(whole,) * 4,
-        scratch_shapes=[
-            pltpu.VMEM((WIDE, WIDE, ZP, C), BF16),
-            pltpu.VMEM((KEYS, C), BF16),
-            pltpu.VMEM((KEYS, C), BF16),
-            pltpu.VMEM((LANES, C), BF16),
-            pltpu.VMEM((LANES, C), BF16),
-            pltpu.VMEM((KEYS, LANES), F32),
-            pltpu.VMEM((KEYS, LANES), F32),
-            pltpu.VMEM((KEYS, LANES), BF16),
-            pltpu.VMEM((KEYS, LANES), BF16),
-            pltpu.VMEM((KEYS, 2 * C), BF16),
-        ],
-        compiler_params=pltpu.CompilerParams(vmem_limit_bytes=40 * 1024 * 1024),
-    )(own, ylo, yhi, xlo, xhi, cot, wqkv, wout)
+        kernel,
+        out_shape=tuple(jax.ShapeDtypeStruct(shape, kind) for shape, kind in outs),
+        in_specs=[whole] * len(args),
+        out_specs=(whole,) * len(outs),
+        scratch_shapes=[pltpu.VMEM(shape, kind) for shape, kind in scratch],
+        cost_estimate=pl.CostEstimate(flops=flops, bytes_accessed=4 * 2**20, transcendentals=0),
+        compiler_params=pltpu.CompilerParams(vmem_limit_bytes=mib * 2**20),
+    )(*args)
+
+
+NC_ = CELLS * ROWS
+NO_ = 2 * RADIUS * ROWS
+
+
+def centre(own, ylo, yhi, cot, wqkv, wout):
+    outs = (
+        ((CELLS, WIDE, ZP, C), BF16),
+        ((LANES, C), BF16),
+        ((LANES, C), BF16),
+        ((NC_, C), BF16),
+        ((NC_, C), BF16),
+        ((NC_, LANES), F32),
+        ((NC_, LANES), F32),
+        ((2, LANES), F32),
+    )
+    return kernel_call(centre_kernel, outs, (own, ylo, yhi, cot, wqkv, wout), flops=10**9)
+
+
+def main(own, cot, wqkv, xlo, xhi, held):
+    outs = (
+        ((NC_, 2 * C), BF16),
+        ((NO_, 2 * C), BF16),
+        ((QUERIES, C), BF16),
+        ((2, 8, 128, 128), BF16),
+    )
+    scratch = (
+        ((2 * RADIUS, WIDE, ZP, C), BF16),
+        ((NO_, C), BF16),
+        ((NO_, C), BF16),
+        ((NO_, LANES), F32),
+        ((NO_, LANES), F32),
+        ((NC_, LANES), BF16),
+        ((NO_, LANES), BF16),
+        ((NC_, LANES), BF16),
+        ((NO_, LANES), BF16),
+    )
+    args = (own, cot, wqkv, xlo, xhi, *held)
+    return kernel_call(main_kernel, outs, args, scratch, flops=3 * 10**9)
+
+
+def through_inputs(gkvc, gkvo, grad_query, wqkv):
+    outs = (
+        ((RADIUS, WIDE, ZP, C), BF16),
+        ((CELLS, WIDE, ZP, C), F32),
+        ((RADIUS, WIDE, ZP, C), BF16),
+    )
+    return kernel_call(inputs_kernel, outs, (gkvc, gkvo, grad_query, wqkv), flops=10**9)
+
+
+def local_grads(own, ylo, yhi, xlo, xhi, cot, wqkv, wout):
+    held = centre(own, ylo, yhi, cot, wqkv, wout)
+    gkvc, gkvo, grad_query, dw = main(own, cot, wqkv, xlo, xhi, held)
+    return (*through_inputs(gkvc, gkvo, grad_query, wqkv), dw)
 
 
 def neighbours(easy, hard, axes):

time: 78.6 us -> 77 us (0.980)
  waiting for transfers between devices: 29 us -> 27 us
    ppermute x4, waiting for transfers between devices: 6.33 us -> 2.59 us  [neighbours(): from_far = lax.ppermute(hard, axes, far)]
    ppermute x4, starting transfers between devices: 6.92 us -> 10 us  [neighbours(): from_far = lax.ppermute(hard, axes, far)]
    ppermute x4, waiting for transfers between devices: 0.01 us -> 2.26 us  [neighbours(): return (lax.ppermute(easy, axes, near), from_far)]
    ppermute x4, starting transfers between devices: 5.47 us -> 4.35 us  [neighbours(): return (lax.ppermute(easy, axes, near), from_far)]
    all_to_all x1, starting transfers between devices: 6.21 us -> 5.28 us  [summed_weights(): lax.all_to_all(jnp.broadcast_to(chunk[None], (8, 64, 128)), 'z', 0, 0)]
    ppermute x1, starting transfers between devices: 5.07 us -> 4.2 us  [summed_weights(): other = lax.ppermute(half, 'core', swap)]
    pallas_call x1 -> x3, Pallas kernels: 4.68 us -> 5.34 us  [kernel_call(): pl.pallas_call(kernel, out_shape=tuple((jax.ShapeDtypeStruct(shape, kind)...]
  transfers between devices with their start and end apart: 13 -> 13, of which waited for: 7 -> 9; matrix products, arithmetic and copies ran while one was open for 2% -> 2% of each run, Pallas kernels for 0% -> 2%
where the time goes in v3:
time: 77 us; the launch traced here: 76.6 us
  starting transfers between devices  38 us (49%)
  waiting for transfers between devices  27 us (35%)
  Pallas kernels  6.37 us (8%)
  local copies, waits for them, and re-layouts  3.18 us (4%)
  other arithmetic  1.25 us (2%)
  between operations  0.84 us (1%)
    ppermute x4, starting transfers between devices, neighbours(): from_far = lax.ppermute(hard, axes, far)  10 us
    all_to_all x1, waiting for transfers between devices, summed_weights(): lax.all_to_all(jnp.broadcast_to(chunk[None], (8, 64, 128)), 'z', 0, 0)  7.85 us
    all_to_all x1, waiting for transfers between devices, summed_weights(): chunks = lax.all_to_all(half, PLANE, 0, 0)  7.51 us
    all_to_all x1, starting transfers between devices, summed_weights(): chunks = lax.all_to_all(half, PLANE, 0, 0)  6.48 us
    all_to_all x1, waiting for transfers between devices, summed_weights(): lax.all_to_all(jnp.broadcast_to(chunk[None], (16, 64, 128)), PLANE, 0, 0)  6.11 us
    pallas_call x3, Pallas kernels, kernel_call(): pl.pallas_call(kernel, out_shape=tuple((jax.ShapeDtypeStruct(shape, kind)...  5.34 us
    all_to_all x1, starting transfers between devices, summed_weights(): lax.all_to_all(jnp.broadcast_to(chunk[None], (8, 64, 128)), 'z', 0, 0)  5.28 us
    ppermute x4, starting transfers between devices, neighbours(): return (lax.ppermute(easy, axes, near), from_far)  4.35 us
  transfers between devices with their start and end apart: 13, of which 9 were waited for; matrix products, arithmetic and copies ran while one was open for 2% of the time, Pallas kernels for 2%

profile of v3, /device:TPU:1, one launch (start us, length us, event | category | flops | bytes accessed | tf_op | source)
XLA Modules:
  0.0 76.6 jit_solution(1383391153533513266)
XLA Ops:
  0.6 0.9 %copy.17.own = bf16[4,4,14,256]{3,2,1,0:T(8,128)(2,1)S(1)} copy(bf16[4,4,14,256]{3,1,2,0:T(4,128)(2,1)} %param.4) | data formatting | bytes 229376 | tf_op args[0]
  1.6 0.0 copy-start
  1.6 0.0 copy-start.1
  1.6 0.0 copy-start.2
  1.6 7.4 %collective-permute-start = (bf16[4,3,14,256]{3,2,1,0:T(8,128)(2,1)S(1)}, bf16[4,3,14,256]{3,2,1,0:T(8,128)(2,1)S(1)}, u32[]{:S(2)}, u32[]{:S(2)}) collective-permute-start(bf16[4,3,14,256]{3,2,1,0:T(8,128)(2,1)S(1)} %get-tuple-element.59), channel_id=1, source_target_pairs={{0,15},{1,2},{2,1},{3,4},{4,3},{5,6},{6,5},{7,8},{8,7},{9,10},{10,... | collective-permute-start | bytes 258056 | tf_op jit(solution)/shard_map/ppermute | solution.py:213
  9.1 0.0 collective-permute-start.1
  9.1 2.5 %collective-permute-done = bf16[4,3,14,256]{3,2,1,0:T(8,128)(2,1)S(1)} collective-permute-done((bf16[4,3,14,256]{3,2,1,0:T(8,128)(2,1)S(1)}, bf16[4,3,14,256]{3,2,1,0:T(8,128)(2,1)S(1)}, u32[]{:S(2)}, u32[]{:S(2)}) %collective-permute-start) | collective-permute-done | bytes 86048 | tf_op jit(solution)/shard_map/ppermute | solution.py:213
  11.6 2.1 %collective-permute-done.1 = bf16[4,3,14,256]{3,2,1,0:T(8,128)(2,1)S(1)} collective-permute-done((bf16[4,3,14,256]{3,2,1,0:T(8,128)(2,1)S(1)}, bf16[4,3,14,256]{3,2,1,0:T(8,128)(2,1)S(1)}, u32[]{:S(2)}, u32[]{:S(2)}) %collective-permute-start.1) | collective-permute-done | bytes 86048 | tf_op jit(solution)/shard_map/ppermute | solution.py:214
  13.7 0.1 pad_maximum_fusion
  13.8 2.5 %collective-permute-start.2 = (bf16[3,10,14,256]{3,2,1,0:T(8,128)(2,1)S(1)}, bf16[3,10,14,256]{3,2,1,0:T(8,128)(2,1)S(1)}, u32[]{:S(2)}, u32[]{:S(2)}) collective-permute-start(bf16[3,10,14,256]{3,2,1,0:T(8,128)(2,1)S(1)} %get-tuple-element.54), channel_id=1, source_target_pairs={{0,240},{16,32},{32,16},{48,64},{64,48},{80,96},{96,80},{112,128},... | collective-permute-start | bytes 645128 | tf_op jit(solution)/shard_map/ppermute | solution.py:213
  16.3 2.9 %collective-permute-start.3 = (bf16[3,10,14,256]{3,2,1,0:T(8,128)(2,1)S(1)}, bf16[3,10,14,256]{3,2,1,0:T(8,128)(2,1)S(1)}, u32[]{:S(2)}, u32[]{:S(2)}) collective-permute-start(bf16[3,10,14,256]{3,2,1,0:T(8,128)(2,1)S(1)} %get-tuple-element.53), channel_id=1, source_target_pairs={{0,16},{16,0},{32,48},{48,32},{64,80},{80,64},{96,112},{112,96},{1... | collective-permute-start | bytes 645128 | tf_op jit(solution)/shard_map/ppermute | solution.py:214
  19.2 0.0 copy-done
  19.2 0.0 copy-done.1
  19.2 0.0 copy-done.2
  19.2 0.9 %shard_map.67 = (bf16[4,10,16,256]{3,2,1,0:T(8,128)(2,1)S(1)}, bf16[512,256]{1,0:T(8,128)(2,1)S(1)}, bf16[512,256]{1,0:T(8,128)(2,1)S(1)}, bf16[640,256]{1,0:T(8...) custom-call(bf16[4,4,14,256]{3,2,1,0:T(8,128)(2,1)S(1)} %copy.17.own, ...), custom_call_target="tpu_custom_call" | custom-call | flops 1000000000 | bytes 4194304 | tf_op jit(solution)/shard_map/pallas_call | solution.py:143
  20.1 0.1 collective-permute-done.2
  20.2 0.1 collective-permute-done.3
  20.4 3.8 %shard_map.68 = (bf16[640,512]{1,0:T(8,128)(2,1)S(1)}, bf16[960,512]{1,0:T(8,128)(2,1)S(1)}, bf16[128,256]{1,0:T(8,128)(2,1)S(1)}, bf16[2,8,128,128]{3,2,1,0:T(8,128)(2,1)S(1)}) custom-call(bf16[4,4,14,256]{3,2,1,0:T(8,128)(2,1)S(1)} %copy.17.own, bf16[4,4,8,256]{3,2,1,0:T(8,128)(2,1)S(1)} %copy-done.2, bf16[256,768]{1,0:T(8,128)(2,1)S(1)} %copy-done, ...), custom_call_target="tpu_custom_call" | custom-call | flops 3000000000 | bytes 4194304 | tf_op jit(solution)/shard_map/pallas_call | solution.py:143
  24.2 4.1 %collective-permute-start.8 = (bf16[16,64,128]{2,1,0:T(8,128)(2,1)S(1)}, bf16[16,64,128]{2,1,0:T(8,128)(2,1)S(1)}, u32[]{:S(2)}, u32[]{:S(2)}) collective-permute-start(bf16[16,64,128]{2,1,0:T(8,128)(2,1)S(1)} %dynamic-slice_bitcast_fusion), channel_id=1, source_target_pairs={{0,16},{16,0},{1,17},{17,1},{2,18},{18,2},{3,19},{19,3},{4,20},{20... | collective-permute-start | bytes 786440 | tf_op jit(solution)/shard_map/ppermute | solution.py:265
  28.3 0.6 shard_map.69
  29.0 0.1 collective-permute-start.4
  29.1 0.1 collective-permute-start.5
  29.2 0.3 collective-permute-done.8
  29.5 0.8 %fusion = bf16[16,64,128]{2,1,0:T(8,128)(2,1)} fusion(bf16[16,64,128]{2,1,0:T(8,128)(2,1)S(1)} %collective-permute-done.8, bf16[2,16,64,128]{3,2,1,0:T(8,128)(2,1)S(1)} %bitcast.10, s32[]{:T(128)S(6)} %select_n.120), kind=kLoop, calls=%fused_computation.2 | loop fusion | flops 524288 | bytes 786436 | tf_op jit(solution)/shard_map/convert_element_type | solution.py:265
  30.3 6.5 %all-to-all-start = ((bf16[16,64,128]{2,1,0:T(8,128)(2,1)}), bf16[16,64,128]{2,1,0:T(8,128)(2,1)S(1)}, u32[]{:S(2)}, u32[]{:S(2)}) async-start(bf16[16,64,128]{2,1,0:T(8,128)(2,1)} %fusion), calls=%async_computation | async-start | bytes 524288 | tf_op jit(solution)/shard_map/all_to_all | solution.py:266
  36.8 0.0 collective-permute-done.4
  36.8 0.0 collective-permute-done.5
  36.8 7.5 %all-to-all-done = bf16[16,64,128]{2,1,0:T(8,128)(2,1)S(1)} async-done(((bf16[16,64,128]{2,1,0:T(8,128)(2,1)}), bf16[16,64,128]{2,1,0:T(8,128)(2,1)S(1)}, u32[]{:S(2)}, u32[]{:S(2)}) %all-to-all-start) | async-done | bytes 262176 | tf_op jit(solution)/shard_map/all_to_all | solution.py:266
  44.4 0.7 broadcast_in_dim.4
  45.1 5.3 %all-to-all-start.1 = ((bf16[8,64,128]{2,1,0:T(8,128)(2,1)}), bf16[8,64,128]{2,1,0:T(8,128)(2,1)S(1)}, u32[]{:S(2)}, u32[]{:S(2)}) async-start(bf16[8,64,128]{2,1,0:T(8,128)(2,1)} %broadcast_in_dim.4), calls=%async_computation.1 | async-start | bytes 262144 | tf_op jit(solution)/shard_map/all_to_all | solution.py:268
  50.3 0.1 fusion.3
  50.5 7.8 %all-to-all-done.1 = bf16[8,64,128]{2,1,0:T(8,128)(2,1)S(1)} async-done(((bf16[8,64,128]{2,1,0:T(8,128)(2,1)}), bf16[8,64,128]{2,1,0:T(8,128)(2,1)S(1)}, u32[]{:S(2)}, u32[]{:S(2)}) %all-to-all-start.1) | async-done | bytes 131104 | tf_op jit(solution)/shard_map/all_to_all | solution.py:268
  58.4 0.8 broadcast_in_dim.5
  59.1 3.5 %all-to-all-start.2 = ((bf16[16,64,128]{2,1,0:T(8,128)(2,1)}), bf16[16,64,128]{2,1,0:T(8,128)(2,1)S(1)}, u32[]{:S(2)}, u32[]{:S(2)}) async-start(bf16[16,64,128]{2,1,0:T(8,128)(2,1)} %broadcast_in_dim.5), calls=%async_computation.2 | async-start | bytes 524288 | tf_op jit(solution)/shard_map/all_to_all | solution.py:270
  62.7 1.4 %collective-permute-start.6 = (bf16[4,3,16,256]{3,2,1,0:T(8,128)(2,1)S(1)}, bf16[4,3,16,256]{3,2,1,0:T(8,128)(2,1)S(1)}, u32[]{:S(2)}, u32[]{:S(2)}) collective-permute-start(bf16[4,3,16,256]{3,2,1,0:T(8,128)(2,1)S(1)} %get-tuple-element.51), channel_id=1, source_target_pairs={{0,1},{1,0},{2,3},{3,2},{4,5},{5,4},{6,7},{7,6},{8,9},{9,8},{10,11... | collective-permute-start | bytes 294920 | tf_op jit(solution)/shard_map/ppermute | solution.py:214
  64.0 0.0 collective-permute-start.7
  64.1 6.1 %all-to-all-done.2 = bf16[16,64,128]{2,1,0:T(8,128)(2,1)S(1)} async-done(((bf16[16,64,128]{2,1,0:T(8,128)(2,1)}), bf16[16,64,128]{2,1,0:T(8,128)(2,1)S(1)}, u32[]{:S(2)}, u32[]{:S(2)}) %all-to-all-start.2) | async-done | bytes 262176 | tf_op jit(solution)/shard_map/all_to_all | solution.py:270
  70.2 4.2 %collective-permute-start.9 = (bf16[16,64,128]{2,1,0:T(8,128)(2,1)S(1)}, bf16[16,64,128]{2,1,0:T(8,128)(2,1)S(1)}, u32[]{:S(2)}, u32[]{:S(2)}) collective-permute-start(bf16[16,64,128]{2,1,0:T(8,128)(2,1)S(1)} %all-to-all-done.2), channel_id=1, source_target_pairs={{0,16},{16,0},{1,17},{17,1},{2,18},{18,2},{3,19},{19,3},{4,20},{20... | collective-permute-start | bytes 786440 | tf_op jit(solution)/shard_map/ppermute | solution.py:271
  74.4 0.0 collective-permute-done.6
  74.4 0.0 collective-permute-done.7
  74.4 0.7 copy.18
  75.2 0.4 collective-permute-done.9
  75.5 1.0 %shard_map.70 = (f32[256,768]{1,0:T(8,128)}, f32[256,256]{1,0:T(8,128)}) custom-call(bf16[8,128,128]{2,1,0:T(8,128)(2,1)S(1)} %bitcast.8, bf16[8,128,128]{2,1,0:T(8,128)(2,1)S(1)} %bitcast.11), custom_call_target="tpu_custom_call" | custom-call | tf_op jit(solution)/shard_map/pallas_call | solution.py:245
  (13 shorter events, 0.4 us)
Async XLA Ops:
  1.6 17.6 %copy-start = (bf16[256,768]{1,0:T(8,128)(2,1)S(1)}, bf16[256,768]{1,0:T(8,128)(2,1)}, u32[]{:S(2)}) copy-start(bf16[256,768]{1,0:T(8,128)(2,1)} %wqkv.5) | copy-start | bytes 1179652
  1.6 17.6 %copy-start.1 = (bf16[256,256]{1,0:T(8,128)(2,1)S(1)}, bf16[256,256]{1,0:T(8,128)(2,1)}, u32[]{:S(2)}) copy-start(bf16[256,256]{1,0:T(8,128)(2,1)} %wout.1) | copy-start | bytes 393220
  1.6 17.6 %copy-start.2 = (bf16[4,4,8,256]{3,2,1,0:T(8,128)(2,1)S(1)}, bf16[4,4,8,256]{3,2,1,0:T(8,128)(2,1)}, u32[]{:S(2)}) copy-start(bf16[4,4,8,256]{3,2,1,0:T(8,128)(2,1)} %cot.3) | copy-start | bytes 196612
  1.6 9.9 %collective-permute-start = (bf16[4,3,14,256]{3,2,1,0:T(8,128)(2,1)S(1)}, bf16[4,3,14,256]{3,2,1,0:T(8,128)(2,1)S(1)}, u32[]{:S(2)}, u32[]{:S(2)}) collective-permute-start(bf16[4,3,14,256]{3,2,1,0:T(8,128)(2,1)S(1)} %get-tuple-element.59), channel_id=1, source_target_pairs={{0,15},{1,2},{2,1},{3,4},{4,3},{5,6},{6,5},{7,8},{8,7},{9,10},{10,... | collective-permute-start | bytes 258056 | tf_op jit(solution)/shard_map/ppermute | solution.py:213
  9.1 4.6 %collective-permute-start.1 = (bf16[4,3,14,256]{3,2,1,0:T(8,128)(2,1)S(1)}, bf16[4,3,14,256]{3,2,1,0:T(8,128)(2,1)S(1)}, u32[]{:S(2)}, u32[]{:S(2)}) collective-permute-start(bf16[4,3,14,256]{3,2,1,0:T(8,128)(2,1)S(1)} %get-tuple-element.60), channel_id=1, source_target_pairs={{0,1},{1,0},{2,3},{3,2},{4,5},{5,4},{6,7},{7,6},{8,9},{9,8},{10,11... | collective-permute-start | bytes 258056 | tf_op jit(solution)/shard_map/ppermute | solution.py:214
  13.8 6.4 %collective-permute-start.2 = (bf16[3,10,14,256]{3,2,1,0:T(8,128)(2,1)S(1)}, bf16[3,10,14,256]{3,2,1,0:T(8,128)(2,1)S(1)}, u32[]{:S(2)}, u32[]{:S(2)}) collective-permute-start(bf16[3,10,14,256]{3,2,1,0:T(8,128)(2,1)S(1)} %get-tuple-element.54), channel_id=1, source_target_pairs={{0,240},{16,32},{32,16},{48,64},{64,48},{80,96},{96,80},{112,128},... | collective-permute-start | bytes 645128 | tf_op jit(solution)/shard_map/ppermute | solution.py:213
  16.3 4.0 %collective-permute-start.3 = (bf16[3,10,14,256]{3,2,1,0:T(8,128)(2,1)S(1)}, bf16[3,10,14,256]{3,2,1,0:T(8,128)(2,1)S(1)}, u32[]{:S(2)}, u32[]{:S(2)}) collective-permute-start(bf16[3,10,14,256]{3,2,1,0:T(8,128)(2,1)S(1)} %get-tuple-element.53), channel_id=1, source_target_pairs={{0,16},{16,0},{32,48},{48,32},{64,80},{80,64},{96,112},{112,96},{1... | collective-permute-start | bytes 645128 | tf_op jit(solution)/shard_map/ppermute | solution.py:214
  24.2 5.3 %collective-permute-start.8 = (bf16[16,64,128]{2,1,0:T(8,128)(2,1)S(1)}, bf16[16,64,128]{2,1,0:T(8,128)(2,1)S(1)}, u32[]{:S(2)}, u32[]{:S(2)}) collective-permute-start(bf16[16,64,128]{2,1,0:T(8,128)(2,1)S(1)} %dynamic-slice_bitcast_fusion), channel_id=1, source_target_pairs={{0,16},{16,0},{1,17},{17,1},{2,18},{18,2},{3,19},{19,3},{4,20},{20... | collective-permute-start | bytes 786440 | tf_op jit(solution)/shard_map/ppermute | solution.py:265
  29.0 7.7 %collective-permute-start.4 = (bf16[3,10,16,256]{3,2,1,0:T(8,128)(2,1)S(1)}, bf16[3,10,16,256]{3,2,1,0:T(8,128)(2,1)S(1)}, u32[]{:S(2)}, u32[]{:S(2)}) collective-permute-start(bf16[3,10,16,256]{3,2,1,0:T(8,128)(2,1)S(1)} %get-tuple-element.47), channel_id=1, source_target_pairs={{0,16},{16,0},{32,48},{48,32},{64,80},{80,64},{96,112},{112,96},{1... | collective-permute-start | bytes 737288 | tf_op jit(solution)/shard_map/ppermute | solution.py:214
  29.1 7.6 %collective-permute-start.5 = (bf16[3,10,16,256]{3,2,1,0:T(8,128)(2,1)S(1)}, bf16[3,10,16,256]{3,2,1,0:T(8,128)(2,1)S(1)}, u32[]{:S(2)}, u32[]{:S(2)}) collective-permute-start(bf16[3,10,16,256]{3,2,1,0:T(8,128)(2,1)S(1)} %get-tuple-element.48), channel_id=1, source_target_pairs={{0,240},{16,32},{32,16},{48,64},{64,48},{80,96},{96,80},{112,128},... | collective-permute-start | bytes 737288 | tf_op jit(solution)/shard_map/ppermute | solution.py:213
  30.3 14.1 %all-to-all-start = ((bf16[16,64,128]{2,1,0:T(8,128)(2,1)}), bf16[16,64,128]{2,1,0:T(8,128)(2,1)S(1)}, u32[]{:S(2)}, u32[]{:S(2)}) async-start(bf16[16,64,128]{2,1,0:T(8,128)(2,1)} %fusion), calls=%async_computation | async-start | bytes 524288 | tf_op jit(solution)/shard_map/all_to_all | solution.py:266
  45.1 13.3 %all-to-all-start.1 = ((bf16[8,64,128]{2,1,0:T(8,128)(2,1)}), bf16[8,64,128]{2,1,0:T(8,128)(2,1)S(1)}, u32[]{:S(2)}, u32[]{:S(2)}) async-start(bf16[8,64,128]{2,1,0:T(8,128)(2,1)} %broadcast_in_dim.4), calls=%async_computation.1 | async-start | bytes 262144 | tf_op jit(solution)/shard_map/all_to_all | solution.py:268
  59.1 11.1 %all-to-all-start.2 = ((bf16[16,64,128]{2,1,0:T(8,128)(2,1)}), bf16[16,64,128]{2,1,0:T(8,128)(2,1)S(1)}, u32[]{:S(2)}, u32[]{:S(2)}) async-start(bf16[16,64,128]{2,1,0:T(8,128)(2,1)} %broadcast_in_dim.5), calls=%async_computation.2 | async-start | bytes 524288 | tf_op jit(solution)/shard_map/all_to_all | solution.py:270
  62.7 11.7 %collective-permute-start.6 = (bf16[4,3,16,256]{3,2,1,0:T(8,128)(2,1)S(1)}, bf16[4,3,16,256]{3,2,1,0:T(8,128)(2,1)S(1)}, u32[]{:S(2)}, u32[]{:S(2)}) collective-permute-start(bf16[4,3,16,256]{3,2,1,0:T(8,128)(2,1)S(1)} %get-tuple-element.51), channel_id=1, source_target_pairs={{0,1},{1,0},{2,3},{3,2},{4,5},{5,4},{6,7},{7,6},{8,9},{9,8},{10,11... | collective-permute-start | bytes 294920 | tf_op jit(solution)/shard_map/ppermute | solution.py:214
  64.0 10.3 %collective-permute-start.7 = (bf16[4,3,16,256]{3,2,1,0:T(8,128)(2,1)S(1)}, bf16[4,3,16,256]{3,2,1,0:T(8,128)(2,1)S(1)}, u32[]{:S(2)}, u32[]{:S(2)}) collective-permute-start(bf16[4,3,16,256]{3,2,1,0:T(8,128)(2,1)S(1)} %get-tuple-element.52), channel_id=1, source_target_pairs={{0,15},{1,2},{2,1},{3,4},{4,3},{5,6},{6,5},{7,8},{8,7},{9,10},{10,... | collective-permute-start | bytes 294920 | tf_op jit(solution)/shard_map/ppermute | solution.py:213
  70.2 5.4 %collective-permute-start.9 = (bf16[16,64,128]{2,1,0:T(8,128)(2,1)S(1)}, bf16[16,64,128]{2,1,0:T(8,128)(2,1)S(1)}, u32[]{:S(2)}, u32[]{:S(2)}) collective-permute-start(bf16[16,64,128]{2,1,0:T(8,128)(2,1)S(1)} %all-to-all-done.2), channel_id=1, source_target_pairs={{0,16},{16,0},{1,17},{17,1},{2,18},{18,2},{3,19},{19,3},{4,20},{20... | collective-permute-start | bytes 786440 | tf_op jit(solution)/shard_map/ppermute | solution.py:271

commit v4 on v3

--- a/solution.py
+++ b/solution.py
@@ -61,11 +61,20 @@
 OUTER = [*range(RADIUS), *range(RADIUS + CELLS, WIDE)]
 
 
+def rims_kernel(inputs, own, near, far):
+    for x in range(CELLS):
+        block = jnp.swapaxes(inputs[x].astype(F32), 0, 1)
+        filled = jnp.concatenate([block, jnp.zeros((CELLS, ZP - ZE, C), F32)], axis=1)
+        own[x] = filled.astype(BF16)
+    odd = lax.axis_index("xl")
+    near[...] = own[:, pl.ds(1 - odd, RADIUS)]
+    far[...] = own[:, pl.ds(odd, RADIUS)]
+
+
 def centre_kernel(own, ylo, yhi, cot, wqkv, wout, xs, qbd, gabd, ks, vs, es, gps, sums):
-    xs[...] = jnp.zeros_like(xs)
-    xs[:, 0:RADIUS, 0:ZE, :] = ylo[...]
-    xs[:, RADIUS : RADIUS + CELLS, 0:ZE, :] = own[...]
-    xs[:, RADIUS + CELLS :, 0:ZE, :] = yhi[...]
+    xs[:, 0:RADIUS] = ylo[...]
+    xs[:, RADIUS : RADIUS + CELLS] = own[...]
+    xs[:, RADIUS + CELLS :] = yhi[...]
     inner = own[...].astype(F32)[:, :, RADIUS : RADIUS + Z, :].reshape(QUERIES, C).astype(BF16)
     cot2 = cot[...].astype(F32).reshape(QUERIES, C).astype(BF16)
     query = mm(inner, wqkv[:, :C]).astype(BF16).astype(F32) * HD ** (-0.5)
@@ -87,9 +96,8 @@
     gkvc, gkvo, grad_query, dw,
     xo, ko, vo, eo, gpo, pbc, pbo, dsc, dso,
 ):
-    xo[...] = jnp.zeros_like(xo)
-    xo[0:RADIUS, :, 0:ZE, :] = xlo[...]
-    xo[RADIUS:, :, 0:ZE, :] = xhi[...]
+    xo[0:RADIUS] = xlo[...]
+    xo[RADIUS:] = xhi[...]
     exp_sum, weighted = forward(
         xo[...].reshape(-1, C), OUTER, wqkv[:, C:], qbd[...], gabd[...], ko, vo, eo, gpo
     )
@@ -116,11 +124,12 @@
     inner = own[...].astype(F32)[:, :, RADIUS : RADIUS + Z, :].reshape(QUERIES, C).astype(BF16)
     cot2 = cot[...].astype(F32).reshape(QUERIES, C).astype(BF16)
     attended = over_keys(((vc, pbc), (vo, pbo))).astype(BF16)
+    grad_q = over_keys(((kc, dsc), (ko, dso))) * HD ** (-0.5)
+    dw_kv = mm(xc[...].reshape(-1, C), gkvc[...], TN) + mm(xo[...].reshape(-1, C), gkvo[...], TN)
+    grad_q = grad_q.T.astype(BF16)
+    grad_query[...] = grad_q
     dw_out = mm(attended, cot2).astype(BF16)
-    grad_q = (over_keys(((kc, dsc), (ko, dso))) * HD ** (-0.5)).T.astype(BF16)
-    grad_query[...] = grad_q
     dw_q = mm(inner, grad_q, TN).astype(BF16)
-    dw_kv = mm(xc[...].reshape(-1, C), gkvc[...], TN) + mm(xo[...].reshape(-1, C), gkvo[...], TN)
     slot = 0
     for part in (dw_q, dw_kv.astype(BF16), dw_out):
         for start in range(0, part.shape[1], 128):
@@ -200,18 +209,31 @@
     return kernel_call(inputs_kernel, outs, (gkvc, gkvo, grad_query, wqkv), flops=10**9)
 
 
+def own_rims(inputs):
+    rim = ((CELLS, RADIUS, ZP, C), BF16)
+    outs = (((CELLS, CELLS, ZP, C), BF16), rim, rim)
+    return kernel_call(rims_kernel, outs, (inputs.transpose(0, 2, 1, 3),), mib=4)
+
+
 def local_grads(own, ylo, yhi, xlo, xhi, cot, wqkv, wout):
     held = centre(own, ylo, yhi, cot, wqkv, wout)
     gkvc, gkvo, grad_query, dw = main(own, cot, wqkv, xlo, xhi, held)
     return (*through_inputs(gkvc, gkvo, grad_query, wqkv), dw)
 
 
+def to_near(block, axes):
+    return lax.ppermute(block, axes, [(i, i ^ 1) for i in range(lax.axis_size(axes))])
+
+
+def to_far(block, axes):
+    size = lax.axis_size(axes)
+    pairs = [(i, (i + 1 if i % 2 else i - 1) % size) for i in range(size)]
+    return lax.ppermute(block, axes, pairs)
+
+
 def neighbours(easy, hard, axes):
-    size = lax.axis_size(axes)
-    near = [(i, i ^ 1) for i in range(size)]
-    far = [(i, (i + 1 if i % 2 else i - 1) % size) for i in range(size)]
-    from_far = lax.ppermute(hard, axes, far)
-    return lax.ppermute(easy, axes, near), from_far
+    from_far = to_far(hard, axes)
+    return to_near(easy, axes), from_far
 
 
 def exchanged(low, high, axes):
@@ -228,7 +250,7 @@
     return jnp.where(odd == 0, far, near), jnp.where(odd == 0, near, far)
 
 
-def place_kernel(half, other, wqkv, wout):
+def last_kernel(half, other, middle, before, after, wqkv, wout, grads):
     core = lax.axis_index("core")
     for part, place in ((half, core), (other, 1 - core)):
         rows = pl.ds(pl.multiple_of(place * 128, 128), 128)
@@ -238,17 +260,31 @@
                 wqkv[rows, slot * 128 : (slot + 1) * 128] = tile
             else:
                 wout[rows, (slot - 6) * 128 : (slot - 5) * 128] = tile
-
-
-def placed(half, other):
+    columns = []
+    for y in range(CELLS):
+        column = middle[:, y]
+        if y < RADIUS:
+            column += before[:, y].astype(F32)
+        if y >= CELLS - RADIUS:
+            column += after[:, y - CELLS + RADIUS].astype(F32)
+        columns.append(column[:, :ZE])
+    grads[...] = jnp.stack(columns, axis=2).astype(BF16)
+
+
+def last(half, other, middle, before, after):
     whole = pl.BlockSpec(memory_space=pltpu.VMEM)
-    return pl.pallas_call(
-        place_kernel,
-        out_shape=(jax.ShapeDtypeStruct((C, 3 * C), F32), jax.ShapeDtypeStruct((C, C), F32)),
-        in_specs=[whole] * 2,
-        out_specs=(whole,) * 2,
-        compiler_params=pltpu.CompilerParams(vmem_limit_bytes=8 * 1024 * 1024),
-    )(half.reshape(8, 128, 128), other.reshape(8, 128, 128))
+    wqkv, wout, grads = pl.pallas_call(
+        last_kernel,
+        out_shape=(
+            jax.ShapeDtypeStruct((C, 3 * C), F32),
+            jax.ShapeDtypeStruct((C, C), F32),
+            jax.ShapeDtypeStruct((CELLS, ZE, CELLS, C), BF16),
+        ),
+        in_specs=[whole] * 5,
+        out_specs=(whole,) * 3,
+        compiler_params=pltpu.CompilerParams(vmem_limit_bytes=10 * 2**20),
+    )(half.reshape(8, 128, 128), other.reshape(8, 128, 128), middle, before, after)
+    return grads.transpose(0, 2, 1, 3), wqkv, wout
 
 
 GX = ("xh", "y", "core")
@@ -269,15 +305,18 @@
     chunk = jnp.sum(columns.astype(F32), axis=0).astype(BF16)
     half = lax.all_to_all(jnp.broadcast_to(chunk[None], (16, 64, 128)), PLANE, 0, 0)
     other = lax.ppermute(half, "core", swap)
-    return placed(half, other)
+    return half, other
 
 
 def body(inputs, cotangent, w_qkv, w_out):
-    ylo, yhi = rims(inputs, 1, GY)
-    wide = jnp.concatenate([ylo, inputs, yhi], axis=1)
+    own, near, far = own_rims(inputs)
+    far, near = to_far(far, GY), to_near(near, GY)
+    first = lax.axis_index(GY) % 2 == 0
+    ylo, yhi = jnp.where(first, far, near), jnp.where(first, near, far)
+    wide = jnp.concatenate([ylo, own, yhi], axis=1)
     xlo, xhi = rims(wide, 0, GX)
     grad_lo, grad_mid, grad_hi, dw = local_grads(
-        inputs, ylo, yhi, xlo, xhi, cotangent, w_qkv, w_out
+        own, ylo, yhi, xlo, xhi, cotangent, w_qkv, w_out
     )
     from_before, from_next = exchanged(grad_lo, grad_hi, GX)
     from_before, from_next = from_before.astype(F32), from_next.astype(F32)
@@ -291,16 +330,8 @@
     low = grad_mid[:, :RADIUS].astype(BF16)
     high = grad_mid[:, RADIUS + CELLS :].astype(BF16)
     from_before, from_next = exchanged(low, high, GY)
-    from_before, from_next = from_before.astype(F32), from_next.astype(F32)
-    rest = ((0, 0), (0, 0))
-    grad_inputs = (
-        middle
-        + jnp.pad(from_next, ((0, 0), (CELLS - RADIUS, 0)) + rest)
-        + jnp.pad(from_before, ((0, 0), (0, CELLS - RADIUS)) + rest)
-    )
-    grad_inputs = grad_inputs[:, :, :ZE].astype(BF16)
-    grad_wqkv, grad_wout = summed_weights(dw)
-    return grad_inputs, grad_wqkv, grad_wout
+    half, other = summed_weights(dw)
+    return last(half, other, middle, from_before, from_next)
 
 
 def solution(mesh):

time: 77 us -> 76.7 us (level)
    pallas_call x3 -> x4, Pallas kernels: 5.34 us -> 5.04 us  [kernel_call(): pl.pallas_call(kernel, out_shape=tuple((jax.ShapeDtypeStruct(shape, kind)...]
  transfers between devices with their start and end apart: 13 -> 13, of which waited for: 9 -> 9; matrix products, arithmetic and copies ran while one was open for 2% -> 1% of each run, Pallas kernels for 2% -> 2%
where the time goes in v4:
time: 76.7 us; the launch traced here: 76.2 us
  starting transfers between devices  38.1 us (50%)
  waiting for transfers between devices  27.6 us (36%)
  Pallas kernels  6.11 us (8%)
  local copies, waits for them, and re-layouts  2.42 us (3%)
  other arithmetic  1.19 us (2%)
  between operations  0.81 us (1%)
    ppermute x4, starting transfers between devices, to_far(): return lax.ppermute(block, axes, pairs)  10.8 us
    all_to_all x1, waiting for transfers between devices, summed_weights(): lax.all_to_all(jnp.broadcast_to(chunk[None], (8, 64, 128)), 'z', 0, 0)  7.85 us
    all_to_all x1, waiting for transfers between devices, summed_weights(): chunks = lax.all_to_all(half, PLANE, 0, 0)  7.53 us
    all_to_all x1, starting transfers between devices, summed_weights(): chunks = lax.all_to_all(half, PLANE, 0, 0)  6.48 us
    all_to_all x1, waiting for transfers between devices, summed_weights(): lax.all_to_all(jnp.broadcast_to(chunk[None], (16, 64, 128)), PLANE, 0, 0)  5.98 us
    all_to_all x1, starting transfers between devices, summed_weights(): lax.all_to_all(jnp.broadcast_to(chunk[None], (8, 64, 128)), 'z', 0, 0)  5.26 us
    pallas_call x4, Pallas kernels, kernel_call(): pl.pallas_call(kernel, out_shape=tuple((jax.ShapeDtypeStruct(shape, kind)...  5.04 us
    ppermute x1, starting transfers between devices, summed_weights(): other = lax.ppermute(half, 'core', swap)  4.2 us
  transfers between devices with their start and end apart: 13, of which 9 were waited for; matrix products, arithmetic and copies ran while one was open for 1% of the time, Pallas kernels for 2%

profile of v4, /device:TPU:1, one launch (start us, length us, event | category | flops | bytes accessed | tf_op | source)
XLA Modules:
  0.0 76.2 jit_solution(10917365714633038867)
XLA Ops:
  0.6 0.0 copy-start
  0.6 0.9 %copy-done = bf16[4,4,14,256]{3,1,2,0:T(4,128)(2,1)S(1)} copy-done((bf16[4,4,14,256]{3,1,2,0:T(4,128)(2,1)S(1)}, bf16[4,4,14,256]{3,1,2,0:T(4,128)(2,1)}, u32[]{:S(2)}) %copy-start) | copy-done | bytes 114712
  1.5 0.0 copy-start.1
  1.5 0.0 copy-start.2
  1.5 0.0 copy-start.3
  1.5 0.1 shard_map.67
  1.6 7.4 %collective-permute-start = (bf16[4,3,16,256]{3,2,1,0:T(8,128)(2,1)S(1)}, bf16[4,3,16,256]{3,2,1,0:T(8,128)(2,1)S(1)}, u32[]{:S(2)}, u32[]{:S(2)}) collective-permute-start(bf16[4,3,16,256]{3,2,1,0:T(8,128)(2,1)S(1)} %get-tuple-element.25), channel_id=1, source_target_pairs={{0,15},{1,2},{2,1},{3,4},{4,3},{5,6},{6,5},{7,8},{8,7},{9,10},{10,... | collective-permute-start | bytes 294920 | tf_op jit(solution)/shard_map/ppermute | solution.py:231
  9.0 0.0 collective-permute-start.1
  9.0 2.5 %collective-permute-done = bf16[4,3,16,256]{3,2,1,0:T(8,128)(2,1)S(1)} collective-permute-done((bf16[4,3,16,256]{3,2,1,0:T(8,128)(2,1)S(1)}, bf16[4,3,16,256]{3,2,1,0:T(8,128)(2,1)S(1)}, u32[]{:S(2)}, u32[]{:S(2)}) %collective-permute-start) | collective-permute-done | bytes 98336 | tf_op jit(solution)/shard_map/ppermute | solution.py:231
  11.6 2.1 %collective-permute-done.1 = bf16[4,3,16,256]{3,2,1,0:T(8,128)(2,1)S(1)} collective-permute-done((bf16[4,3,16,256]{3,2,1,0:T(8,128)(2,1)S(1)}, bf16[4,3,16,256]{3,2,1,0:T(8,128)(2,1)S(1)}, u32[]{:S(2)}, u32[]{:S(2)}) %collective-permute-start.1) | collective-permute-done | bytes 98336 | tf_op jit(solution)/shard_map/ppermute | solution.py:225
  13.8 2.5 %collective-permute-start.2 = (bf16[3,10,16,256]{3,2,1,0:T(8,128)(2,1)S(1)}, bf16[3,10,16,256]{3,2,1,0:T(8,128)(2,1)S(1)}, u32[]{:S(2)}, u32[]{:S(2)}) collective-permute-start(bf16[3,10,16,256]{3,2,1,0:T(8,128)(2,1)S(1)} %get-tuple-element.56), channel_id=1, source_target_pairs={{0,240},{16,32},{32,16},{48,64},{64,48},{80,96},{96,80},{112,128},... | collective-permute-start | bytes 737288 | tf_op jit(solution)/shard_map/ppermute | solution.py:231
  16.3 2.9 %collective-permute-start.3 = (bf16[3,10,16,256]{3,2,1,0:T(8,128)(2,1)S(1)}, bf16[3,10,16,256]{3,2,1,0:T(8,128)(2,1)S(1)}, u32[]{:S(2)}, u32[]{:S(2)}) collective-permute-start(bf16[3,10,16,256]{3,2,1,0:T(8,128)(2,1)S(1)} %get-tuple-element.55), channel_id=1, source_target_pairs={{0,16},{16,0},{32,48},{48,32},{64,80},{80,64},{96,112},{112,96},{1... | collective-permute-start | bytes 737288 | tf_op jit(solution)/shard_map/ppermute | solution.py:225
  19.2 0.0 copy-done.1
  19.2 0.0 copy-done.2
  19.2 0.0 copy-done.3
  19.2 0.9 %shard_map.68 = (bf16[4,10,16,256]{3,2,1,0:T(8,128)(2,1)S(1)}, bf16[512,256]{1,0:T(8,128)(2,1)S(1)}, bf16[512,256]{1,0:T(8,128)(2,1)S(1)}, bf16[640,256]{1,0:T(8...) custom-call(bf16[4,4,16,256]{3,2,1,0:T(8,128)(2,1)S(1)} %get-tuple-e, ...), custom_call_target="tpu_custom_call" | custom-call | flops 1000000000 | bytes 4194304 | tf_op jit(solution)/shard_map/pallas_call | solution.py:152
  20.1 0.1 collective-permute-done.2
  20.2 0.1 collective-permute-done.3
  20.3 3.4 %shard_map.69 = (bf16[640,512]{1,0:T(8,128)(2,1)S(1)}, bf16[960,512]{1,0:T(8,128)(2,1)S(1)}, bf16[128,256]{1,0:T(8,128)(2,1)S(1)}, bf16[2,8,128,128]{3,2,1,0:T(8,128)(2,1)S(1)}) custom-call(bf16[4,4,16,256]{3,2,1,0:T(8,128)(2,1)S(1)} %get-tuple-element.24.own, bf16[4,4,8,256]{3,2,1,0:T(8,128)(2,1)S(1)} %copy-done.3, bf16[256,768]{1,0:T(8,128)(2,1)S(1)} %copy-done.1, ...), custom_call_target="tpu_custom_call" | custom-call | flops 3000000000 | bytes 4194304 | tf_op jit(solution)/shard_map/pallas_call | solution.py:152
  23.8 4.1 %collective-permute-start.4 = (bf16[16,64,128]{2,1,0:T(8,128)(2,1)S(1)}, bf16[16,64,128]{2,1,0:T(8,128)(2,1)S(1)}, u32[]{:S(2)}, u32[]{:S(2)}) collective-permute-start(bf16[16,64,128]{2,1,0:T(8,128)(2,1)S(1)} %dynamic-slice_bitcast_fusion), channel_id=1, source_target_pairs={{0,16},{16,0},{1,17},{17,1},{2,18},{18,2},{3,19},{19,3},{4,20},{20... | collective-permute-start | bytes 786440 | tf_op jit(solution)/shard_map/ppermute | solution.py:301
  27.9 0.6 shard_map.70
  28.6 0.1 collective-permute-start.6
  28.7 0.1 collective-permute-start.7
  28.8 0.3 collective-permute-done.4
  29.1 0.8 %fusion = bf16[16,64,128]{2,1,0:T(8,128)(2,1)} fusion(bf16[16,64,128]{2,1,0:T(8,128)(2,1)S(1)} %collective-permute-done.4, bf16[2,16,64,128]{3,2,1,0:T(8,128)(2,1)S(1)} %bitcast.12, s32[]{:T(128)S(6)} %select_n.94), kind=kLoop, calls=%fused_computation.2 | loop fusion | flops 524288 | bytes 786436 | tf_op jit(solution)/shard_map/convert_element_type | solution.py:301
  29.9 6.5 %all-to-all-start = ((bf16[16,64,128]{2,1,0:T(8,128)(2,1)}), bf16[16,64,128]{2,1,0:T(8,128)(2,1)S(1)}, u32[]{:S(2)}, u32[]{:S(2)}) async-start(bf16[16,64,128]{2,1,0:T(8,128)(2,1)} %fusion), calls=%async_computation | async-start | bytes 524288 | tf_op jit(solution)/shard_map/all_to_all | solution.py:302
  36.3 0.0 collective-permute-done.6
  36.4 0.0 collective-permute-done.7
  36.4 7.5 %all-to-all-done = bf16[16,64,128]{2,1,0:T(8,128)(2,1)S(1)} async-done(((bf16[16,64,128]{2,1,0:T(8,128)(2,1)}), bf16[16,64,128]{2,1,0:T(8,128)(2,1)S(1)}, u32[]{:S(2)}, u32[]{:S(2)}) %all-to-all-start) | async-done | bytes 262176 | tf_op jit(solution)/shard_map/all_to_all | solution.py:302
  44.0 0.7 broadcast_in_dim.4
  44.7 5.3 %all-to-all-start.1 = ((bf16[8,64,128]{2,1,0:T(8,128)(2,1)}), bf16[8,64,128]{2,1,0:T(8,128)(2,1)S(1)}, u32[]{:S(2)}, u32[]{:S(2)}) async-start(bf16[8,64,128]{2,1,0:T(8,128)(2,1)} %broadcast_in_dim.4), calls=%async_computation.1 | async-start | bytes 262144 | tf_op jit(solution)/shard_map/all_to_all | solution.py:304
  49.9 0.1 fusion.1
  50.1 7.9 %all-to-all-done.1 = bf16[8,64,128]{2,1,0:T(8,128)(2,1)S(1)} async-done(((bf16[8,64,128]{2,1,0:T(8,128)(2,1)}), bf16[8,64,128]{2,1,0:T(8,128)(2,1)S(1)}, u32[]{:S(2)}, u32[]{:S(2)}) %all-to-all-start.1) | async-done | bytes 131104 | tf_op jit(solution)/shard_map/all_to_all | solution.py:304
  57.9 0.8 broadcast_in_dim.5
  58.7 3.5 %all-to-all-start.2 = ((bf16[16,64,128]{2,1,0:T(8,128)(2,1)}), bf16[16,64,128]{2,1,0:T(8,128)(2,1)S(1)}, u32[]{:S(2)}, u32[]{:S(2)}) async-start(bf16[16,64,128]{2,1,0:T(8,128)(2,1)} %broadcast_in_dim.5), calls=%async_computation.2 | async-start | bytes 524288 | tf_op jit(solution)/shard_map/all_to_all | solution.py:306
  62.3 0.8 collective-permute-start.8
  63.0 0.7 collective-permute-start.9
  63.8 6.0 %all-to-all-done.2 = bf16[16,64,128]{2,1,0:T(8,128)(2,1)S(1)} async-done(((bf16[16,64,128]{2,1,0:T(8,128)(2,1)}), bf16[16,64,128]{2,1,0:T(8,128)(2,1)S(1)}, u32[]{:S(2)}, u32[]{:S(2)}) %all-to-all-start.2) | async-done | bytes 262176 | tf_op jit(solution)/shard_map/all_to_all | solution.py:306
  69.8 4.2 %collective-permute-start.5 = (bf16[16,64,128]{2,1,0:T(8,128)(2,1)S(1)}, bf16[16,64,128]{2,1,0:T(8,128)(2,1)S(1)}, u32[]{:S(2)}, u32[]{:S(2)}) collective-permute-start(bf16[16,64,128]{2,1,0:T(8,128)(2,1)S(1)} %all-to-all-done.2), channel_id=1, source_target_pairs={{0,16},{16,0},{1,17},{17,1},{2,18},{18,2},{3,19},{19,3},{4,20},{20... | collective-permute-start | bytes 786440 | tf_op jit(solution)/shard_map/ppermute | solution.py:307
  74.0 0.0 collective-permute-done.8
  74.0 0.0 collective-permute-done.9
  74.0 1.1 %collective-permute-done.5 = bf16[16,64,128]{2,1,0:T(8,128)(2,1)S(1)} collective-permute-done((bf16[16,64,128]{2,1,0:T(8,128)(2,1)S(1)}, bf16[16,64,128]{2,1,0:T(8,128)(2,1)S(1)}, u32[]{:S(2)}, u32[]{:S(2)}) %collective-permute-start.5) | collective-permute-done | bytes 262176 | tf_op jit(solution)/shard_map/ppermute | solution.py:307
  75.1 1.1 %shard_map.71 = (f32[256,768]{1,0:T(8,128)}, f32[256,256]{1,0:T(8,128)}, bf16[4,14,4,256]{3,2,1,0:T(4,128)(2,1)}) custom-call(bf16[8,128,128]{2,1,0:T(8,128)(2,1)S(1)} %bitcast.10, bf16[8,128,128]{2,1,0:T(8,128)(2,1)S(1)} %bitcast.13, f32[4,4,16,256]{3,2,1,0:T(8,128)S(1)} %slice.14.middle, bf16[4,3,16,256]{3,2,1,0:T(8,128)(2,1)S(1)} %get-tuple-element.58.before, ...), custom_call_target="tpu_custom_call" | custom-call | tf_op jit(solution)/shard_map/pallas_call | solution.py:276
  (12 shorter events, 0.4 us)
Async XLA Ops:
  0.6 0.9 %copy-start = (bf16[4,4,14,256]{3,1,2,0:T(4,128)(2,1)S(1)}, bf16[4,4,14,256]{3,1,2,0:T(4,128)(2,1)}, u32[]{:S(2)}) copy-start(bf16[4,4,14,256]{3,1,2,0:T(4,128)(2,1)} %param.4) | copy-start | bytes 344068
  1.5 17.6 %copy-start.1 = (bf16[256,768]{1,0:T(8,128)(2,1)S(1)}, bf16[256,768]{1,0:T(8,128)(2,1)}, u32[]{:S(2)}) copy-start(bf16[256,768]{1,0:T(8,128)(2,1)} %wqkv.5) | copy-start | bytes 1179652
  1.5 17.6 %copy-start.2 = (bf16[256,256]{1,0:T(8,128)(2,1)S(1)}, bf16[256,256]{1,0:T(8,128)(2,1)}, u32[]{:S(2)}) copy-start(bf16[256,256]{1,0:T(8,128)(2,1)} %wout.1) | copy-start | bytes 393220
  1.5 17.6 %copy-start.3 = (bf16[4,4,8,256]{3,2,1,0:T(8,128)(2,1)S(1)}, bf16[4,4,8,256]{3,2,1,0:T(8,128)(2,1)}, u32[]{:S(2)}) copy-start(bf16[4,4,8,256]{3,2,1,0:T(8,128)(2,1)} %cot.3) | copy-start | bytes 196612
  1.6 9.9 %collective-permute-start = (bf16[4,3,16,256]{3,2,1,0:T(8,128)(2,1)S(1)}, bf16[4,3,16,256]{3,2,1,0:T(8,128)(2,1)S(1)}, u32[]{:S(2)}, u32[]{:S(2)}) collective-permute-start(bf16[4,3,16,256]{3,2,1,0:T(8,128)(2,1)S(1)} %get-tuple-element.25), channel_id=1, source_target_pairs={{0,15},{1,2},{2,1},{3,4},{4,3},{5,6},{6,5},{7,8},{8,7},{9,10},{10,... | collective-permute-start | bytes 294920 | tf_op jit(solution)/shard_map/ppermute | solution.py:231
  9.0 4.6 %collective-permute-start.1 = (bf16[4,3,16,256]{3,2,1,0:T(8,128)(2,1)S(1)}, bf16[4,3,16,256]{3,2,1,0:T(8,128)(2,1)S(1)}, u32[]{:S(2)}, u32[]{:S(2)}) collective-permute-start(bf16[4,3,16,256]{3,2,1,0:T(8,128)(2,1)S(1)} %get-tuple-element.26), channel_id=1, source_target_pairs={{0,1},{1,0},{2,3},{3,2},{4,5},{5,4},{6,7},{7,6},{8,9},{9,8},{10,11... | collective-permute-start | bytes 294920 | tf_op jit(solution)/shard_map/ppermute | solution.py:225
  13.8 6.4 %collective-permute-start.2 = (bf16[3,10,16,256]{3,2,1,0:T(8,128)(2,1)S(1)}, bf16[3,10,16,256]{3,2,1,0:T(8,128)(2,1)S(1)}, u32[]{:S(2)}, u32[]{:S(2)}) collective-permute-start(bf16[3,10,16,256]{3,2,1,0:T(8,128)(2,1)S(1)} %get-tuple-element.56), channel_id=1, source_target_pairs={{0,240},{16,32},{32,16},{48,64},{64,48},{80,96},{96,80},{112,128},... | collective-permute-start | bytes 737288 | tf_op jit(solution)/shard_map/ppermute | solution.py:231
  16.3 4.0 %collective-permute-start.3 = (bf16[3,10,16,256]{3,2,1,0:T(8,128)(2,1)S(1)}, bf16[3,10,16,256]{3,2,1,0:T(8,128)(2,1)S(1)}, u32[]{:S(2)}, u32[]{:S(2)}) collective-permute-start(bf16[3,10,16,256]{3,2,1,0:T(8,128)(2,1)S(1)} %get-tuple-element.55), channel_id=1, source_target_pairs={{0,16},{16,0},{32,48},{48,32},{64,80},{80,64},{96,112},{112,96},{1... | collective-permute-start | bytes 737288 | tf_op jit(solution)/shard_map/ppermute | solution.py:225
  23.8 5.3 %collective-permute-start.4 = (bf16[16,64,128]{2,1,0:T(8,128)(2,1)S(1)}, bf16[16,64,128]{2,1,0:T(8,128)(2,1)S(1)}, u32[]{:S(2)}, u32[]{:S(2)}) collective-permute-start(bf16[16,64,128]{2,1,0:T(8,128)(2,1)S(1)} %dynamic-slice_bitcast_fusion), channel_id=1, source_target_pairs={{0,16},{16,0},{1,17},{17,1},{2,18},{18,2},{3,19},{19,3},{4,20},{20... | collective-permute-start | bytes 786440 | tf_op jit(solution)/shard_map/ppermute | solution.py:301
  28.6 7.7 %collective-permute-start.6 = (bf16[3,10,16,256]{3,2,1,0:T(8,128)(2,1)S(1)}, bf16[3,10,16,256]{3,2,1,0:T(8,128)(2,1)S(1)}, u32[]{:S(2)}, u32[]{:S(2)}) collective-permute-start(bf16[3,10,16,256]{3,2,1,0:T(8,128)(2,1)S(1)} %get-tuple-element.49), channel_id=1, source_target_pairs={{0,16},{16,0},{32,48},{48,32},{64,80},{80,64},{96,112},{112,96},{1... | collective-permute-start | bytes 737288 | tf_op jit(solution)/shard_map/ppermute | solution.py:225
  28.7 7.6 %collective-permute-start.7 = (bf16[3,10,16,256]{3,2,1,0:T(8,128)(2,1)S(1)}, bf16[3,10,16,256]{3,2,1,0:T(8,128)(2,1)S(1)}, u32[]{:S(2)}, u32[]{:S(2)}) collective-permute-start(bf16[3,10,16,256]{3,2,1,0:T(8,128)(2,1)S(1)} %get-tuple-element.50), channel_id=1, source_target_pairs={{0,240},{16,32},{32,16},{48,64},{64,48},{80,96},{96,80},{112,128},... | collective-permute-start | bytes 737288 | tf_op jit(solution)/shard_map/ppermute | solution.py:231
  29.9 14.1 %all-to-all-start = ((bf16[16,64,128]{2,1,0:T(8,128)(2,1)}), bf16[16,64,128]{2,1,0:T(8,128)(2,1)S(1)}, u32[]{:S(2)}, u32[]{:S(2)}) async-start(bf16[16,64,128]{2,1,0:T(8,128)(2,1)} %fusion), calls=%async_computation | async-start | bytes 524288 | tf_op jit(solution)/shard_map/all_to_all | solution.py:302
  44.7 13.2 %all-to-all-start.1 = ((bf16[8,64,128]{2,1,0:T(8,128)(2,1)}), bf16[8,64,128]{2,1,0:T(8,128)(2,1)S(1)}, u32[]{:S(2)}, u32[]{:S(2)}) async-start(bf16[8,64,128]{2,1,0:T(8,128)(2,1)} %broadcast_in_dim.4), calls=%async_computation.1 | async-start | bytes 262144 | tf_op jit(solution)/shard_map/all_to_all | solution.py:304
  58.7 11.1 %all-to-all-start.2 = ((bf16[16,64,128]{2,1,0:T(8,128)(2,1)}), bf16[16,64,128]{2,1,0:T(8,128)(2,1)S(1)}, u32[]{:S(2)}, u32[]{:S(2)}) async-start(bf16[16,64,128]{2,1,0:T(8,128)(2,1)} %broadcast_in_dim.5), calls=%async_computation.2 | async-start | bytes 524288 | tf_op jit(solution)/shard_map/all_to_all | solution.py:306
  62.3 11.7 %collective-permute-start.8 = (bf16[4,3,16,256]{3,2,1,0:T(8,128)(2,1)S(1)}, bf16[4,3,16,256]{3,2,1,0:T(8,128)(2,1)S(1)}, u32[]{:S(2)}, u32[]{:S(2)}) collective-permute-start(bf16[4,3,16,256]{3,2,1,0:T(8,128)(2,1)S(1)} %get-tuple-element.54), channel_id=1, source_target_pairs={{0,15},{1,2},{2,1},{3,4},{4,3},{5,6},{6,5},{7,8},{8,7},{9,10},{10,... | collective-permute-start | bytes 294920 | tf_op jit(solution)/shard_map/ppermute | solution.py:231
  63.0 11.0 %collective-permute-start.9 = (bf16[4,3,16,256]{3,2,1,0:T(8,128)(2,1)S(1)}, bf16[4,3,16,256]{3,2,1,0:T(8,128)(2,1)S(1)}, u32[]{:S(2)}, u32[]{:S(2)}) collective-permute-start(bf16[4,3,16,256]{3,2,1,0:T(8,128)(2,1)S(1)} %get-tuple-element.53), channel_id=1, source_target_pairs={{0,1},{1,0},{2,3},{3,2},{4,5},{5,4},{6,7},{7,6},{8,9},{9,8},{10,11... | collective-permute-start | bytes 294920 | tf_op jit(solution)/shard_map/ppermute | solution.py:225
  69.8 5.4 %collective-permute-start.5 = (bf16[16,64,128]{2,1,0:T(8,128)(2,1)S(1)}, bf16[16,64,128]{2,1,0:T(8,128)(2,1)S(1)}, u32[]{:S(2)}, u32[]{:S(2)}) collective-permute-start(bf16[16,64,128]{2,1,0:T(8,128)(2,1)S(1)} %all-to-all-done.2), channel_id=1, source_target_pairs={{0,16},{16,0},{1,17},{17,1},{2,18},{18,2},{3,19},{19,3},{4,20},{20... | collective-permute-start | bytes 786440 | tf_op jit(solution)/shard_map/ppermute | solution.py:307

commit v5 on v4

--- a/solution.py
+++ b/solution.py
@@ -289,7 +289,7 @@
 
 GX = ("xh", "y", "core")
 GY = ("z", "xl")
-PLANE = ("xh", "y", "xl")
+PLANE = ("xl", "y", "xh")
 
 
 def summed_weights(dw):

time: 76.7 us -> 76.4 us (level)
  no operation moved by 1% of the time
where the time goes in v5:
time: 76.4 us; the launch traced here: 75.9 us
  starting transfers between devices  37.8 us (49%)
  waiting for transfers between devices  27.6 us (36%)
  Pallas kernels  6.11 us (8%)
  local copies, waits for them, and re-layouts  2.42 us (3%)
  other arithmetic  1.19 us (2%)
  between operations  0.81 us (1%)
    ppermute x4, starting transfers between devices, to_far(): return lax.ppermute(block, axes, pairs)  10.6 us
    all_to_all x1, waiting for transfers between devices, summed_weights(): lax.all_to_all(jnp.broadcast_to(chunk[None], (8, 64, 128)), 'z', 0, 0)  7.9 us
    all_to_all x1, waiting for transfers between devices, summed_weights(): chunks = lax.all_to_all(half, PLANE, 0, 0)  7.62 us
    all_to_all x1, starting transfers between devices, summed_weights(): chunks = lax.all_to_all(half, PLANE, 0, 0)  6.48 us
    all_to_all x1, waiting for transfers between devices, summed_weights(): lax.all_to_all(jnp.broadcast_to(chunk[None], (16, 64, 128)), PLANE, 0, 0)  5.88 us
    pallas_call x4, Pallas kernels, kernel_call(): pl.pallas_call(kernel, out_shape=tuple((jax.ShapeDtypeStruct(shape, kind)...  5.04 us
    all_to_all x1, starting transfers between devices, summed_weights(): lax.all_to_all(jnp.broadcast_to(chunk[None], (8, 64, 128)), 'z', 0, 0)  4.79 us
    ppermute x1, starting transfers between devices, summed_weights(): other = lax.ppermute(half, 'core', swap)  4.38 us
  transfers between devices with their start and end apart: 13, of which 9 were waited for; matrix products, arithmetic and copies ran while one was open for 1% of the time, Pallas kernels for 2%

profile of v5, /device:TPU:1, one launch (start us, length us, event | category | flops | bytes accessed | tf_op | source)
XLA Modules:
  0.0 75.9 jit_solution(12976269235293758585)
XLA Ops:
  0.6 0.0 copy-start
  0.6 0.9 %copy-done = bf16[4,4,14,256]{3,1,2,0:T(4,128)(2,1)S(1)} copy-done((bf16[4,4,14,256]{3,1,2,0:T(4,128)(2,1)S(1)}, bf16[4,4,14,256]{3,1,2,0:T(4,128)(2,1)}, u32[]{:S(2)}) %copy-start) | copy-done | bytes 114712
  1.5 0.0 copy-start.1
  1.5 0.0 copy-start.2
  1.5 0.0 copy-start.3
  1.5 0.1 shard_map.67
  1.6 7.4 %collective-permute-start = (bf16[4,3,16,256]{3,2,1,0:T(8,128)(2,1)S(1)}, bf16[4,3,16,256]{3,2,1,0:T(8,128)(2,1)S(1)}, u32[]{:S(2)}, u32[]{:S(2)}) collective-permute-start(bf16[4,3,16,256]{3,2,1,0:T(8,128)(2,1)S(1)} %get-tuple-element.25), channel_id=1, source_target_pairs={{0,15},{1,2},{2,1},{3,4},{4,3},{5,6},{6,5},{7,8},{8,7},{9,10},{10,... | collective-permute-start | bytes 294920 | tf_op jit(solution)/shard_map/ppermute | solution.py:231
  9.0 0.0 collective-permute-start.1
  9.0 2.5 %collective-permute-done = bf16[4,3,16,256]{3,2,1,0:T(8,128)(2,1)S(1)} collective-permute-done((bf16[4,3,16,256]{3,2,1,0:T(8,128)(2,1)S(1)}, bf16[4,3,16,256]{3,2,1,0:T(8,128)(2,1)S(1)}, u32[]{:S(2)}, u32[]{:S(2)}) %collective-permute-start) | collective-permute-done | bytes 98336 | tf_op jit(solution)/shard_map/ppermute | solution.py:231
  11.6 2.1 %collective-permute-done.1 = bf16[4,3,16,256]{3,2,1,0:T(8,128)(2,1)S(1)} collective-permute-done((bf16[4,3,16,256]{3,2,1,0:T(8,128)(2,1)S(1)}, bf16[4,3,16,256]{3,2,1,0:T(8,128)(2,1)S(1)}, u32[]{:S(2)}, u32[]{:S(2)}) %collective-permute-start.1) | collective-permute-done | bytes 98336 | tf_op jit(solution)/shard_map/ppermute | solution.py:225
  13.8 2.5 %collective-permute-start.2 = (bf16[3,10,16,256]{3,2,1,0:T(8,128)(2,1)S(1)}, bf16[3,10,16,256]{3,2,1,0:T(8,128)(2,1)S(1)}, u32[]{:S(2)}, u32[]{:S(2)}) collective-permute-start(bf16[3,10,16,256]{3,2,1,0:T(8,128)(2,1)S(1)} %get-tuple-element.56), channel_id=1, source_target_pairs={{0,240},{16,32},{32,16},{48,64},{64,48},{80,96},{96,80},{112,128},... | collective-permute-start | bytes 737288 | tf_op jit(solution)/shard_map/ppermute | solution.py:231
  16.3 2.9 %collective-permute-start.3 = (bf16[3,10,16,256]{3,2,1,0:T(8,128)(2,1)S(1)}, bf16[3,10,16,256]{3,2,1,0:T(8,128)(2,1)S(1)}, u32[]{:S(2)}, u32[]{:S(2)}) collective-permute-start(bf16[3,10,16,256]{3,2,1,0:T(8,128)(2,1)S(1)} %get-tuple-element.55), channel_id=1, source_target_pairs={{0,16},{16,0},{32,48},{48,32},{64,80},{80,64},{96,112},{112,96},{1... | collective-permute-start | bytes 737288 | tf_op jit(solution)/shard_map/ppermute | solution.py:225
  19.2 0.0 copy-done.1
  19.2 0.0 copy-done.2
  19.2 0.0 copy-done.3
  19.2 0.9 %shard_map.68 = (bf16[4,10,16,256]{3,2,1,0:T(8,128)(2,1)S(1)}, bf16[512,256]{1,0:T(8,128)(2,1)S(1)}, bf16[512,256]{1,0:T(8,128)(2,1)S(1)}, bf16[640,256]{1,0:T(8...) custom-call(bf16[4,4,16,256]{3,2,1,0:T(8,128)(2,1)S(1)} %get-tuple-e, ...), custom_call_target="tpu_custom_call" | custom-call | flops 1000000000 | bytes 4194304 | tf_op jit(solution)/shard_map/pallas_call | solution.py:152
  20.1 0.1 collective-permute-done.2
  20.2 0.1 collective-permute-done.3
  20.3 3.4 %shard_map.69 = (bf16[640,512]{1,0:T(8,128)(2,1)S(1)}, bf16[960,512]{1,0:T(8,128)(2,1)S(1)}, bf16[128,256]{1,0:T(8,128)(2,1)S(1)}, bf16[2,8,128,128]{3,2,1,0:T(8,128)(2,1)S(1)}) custom-call(bf16[4,4,16,256]{3,2,1,0:T(8,128)(2,1)S(1)} %get-tuple-element.24.own, bf16[4,4,8,256]{3,2,1,0:T(8,128)(2,1)S(1)} %copy-done.3, bf16[256,768]{1,0:T(8,128)(2,1)S(1)} %copy-done.1, ...), custom_call_target="tpu_custom_call" | custom-call | flops 3000000000 | bytes 4194304 | tf_op jit(solution)/shard_map/pallas_call | solution.py:152
  23.8 4.1 %collective-permute-start.4 = (bf16[16,64,128]{2,1,0:T(8,128)(2,1)S(1)}, bf16[16,64,128]{2,1,0:T(8,128)(2,1)S(1)}, u32[]{:S(2)}, u32[]{:S(2)}) collective-permute-start(bf16[16,64,128]{2,1,0:T(8,128)(2,1)S(1)} %dynamic-slice_bitcast_fusion), channel_id=1, source_target_pairs={{0,16},{16,0},{1,17},{17,1},{2,18},{18,2},{3,19},{19,3},{4,20},{20... | collective-permute-start | bytes 786440 | tf_op jit(solution)/shard_map/ppermute | solution.py:301
  27.9 0.6 shard_map.70
  28.6 0.1 collective-permute-start.6
  28.7 0.1 collective-permute-start.7
  28.8 0.3 collective-permute-done.4
  29.1 0.8 %fusion = bf16[16,64,128]{2,1,0:T(8,128)(2,1)} fusion(bf16[16,64,128]{2,1,0:T(8,128)(2,1)S(1)} %collective-permute-done.4, bf16[2,16,64,128]{3,2,1,0:T(8,128)(2,1)S(1)} %bitcast.12, s32[]{:T(128)S(6)} %select_n.94), kind=kLoop, calls=%fused_computation.2 | loop fusion | flops 524288 | bytes 786436 | tf_op jit(solution)/shard_map/convert_element_type | solution.py:301
  29.9 6.5 %all-to-all-start = ((bf16[16,64,128]{2,1,0:T(8,128)(2,1)}), bf16[16,64,128]{2,1,0:T(8,128)(2,1)S(1)}, u32[]{:S(2)}, u32[]{:S(2)}) async-start(bf16[16,64,128]{2,1,0:T(8,128)(2,1)} %fusion), calls=%async_computation | async-start | bytes 524288 | tf_op jit(solution)/shard_map/all_to_all | solution.py:302
  36.3 0.0 collective-permute-done.6
  36.4 0.0 collective-permute-done.7
  36.4 7.6 %all-to-all-done = bf16[16,64,128]{2,1,0:T(8,128)(2,1)S(1)} async-done(((bf16[16,64,128]{2,1,0:T(8,128)(2,1)}), bf16[16,64,128]{2,1,0:T(8,128)(2,1)S(1)}, u32[]{:S(2)}, u32[]{:S(2)}) %all-to-all-start) | async-done | bytes 262176 | tf_op jit(solution)/shard_map/all_to_all | solution.py:302
  44.1 0.7 broadcast_in_dim.4
  44.8 4.8 %all-to-all-start.1 = ((bf16[8,64,128]{2,1,0:T(8,128)(2,1)}), bf16[8,64,128]{2,1,0:T(8,128)(2,1)S(1)}, u32[]{:S(2)}, u32[]{:S(2)}) async-start(bf16[8,64,128]{2,1,0:T(8,128)(2,1)} %broadcast_in_dim.4), calls=%async_computation.1 | async-start | bytes 262144 | tf_op jit(solution)/shard_map/all_to_all | solution.py:304
  49.5 0.1 fusion.1
  49.7 7.9 %all-to-all-done.1 = bf16[8,64,128]{2,1,0:T(8,128)(2,1)S(1)} async-done(((bf16[8,64,128]{2,1,0:T(8,128)(2,1)}), bf16[8,64,128]{2,1,0:T(8,128)(2,1)S(1)}, u32[]{:S(2)}, u32[]{:S(2)}) %all-to-all-start.1) | async-done | bytes 131104 | tf_op jit(solution)/shard_map/all_to_all | solution.py:304
  57.6 0.8 broadcast_in_dim.5
  58.4 3.5 %all-to-all-start.2 = ((bf16[16,64,128]{2,1,0:T(8,128)(2,1)}), bf16[16,64,128]{2,1,0:T(8,128)(2,1)S(1)}, u32[]{:S(2)}, u32[]{:S(2)}) async-start(bf16[16,64,128]{2,1,0:T(8,128)(2,1)} %broadcast_in_dim.5), calls=%async_computation.2 | async-start | bytes 524288 | tf_op jit(solution)/shard_map/all_to_all | solution.py:306
  61.9 0.6 collective-permute-start.8
  62.5 0.9 %collective-permute-start.9 = (bf16[4,3,16,256]{3,2,1,0:T(8,128)(2,1)S(1)}, bf16[4,3,16,256]{3,2,1,0:T(8,128)(2,1)S(1)}, u32[]{:S(2)}, u32[]{:S(2)}) collective-permute-start(bf16[4,3,16,256]{3,2,1,0:T(8,128)(2,1)S(1)} %get-tuple-element.53), channel_id=1, source_target_pairs={{0,1},{1,0},{2,3},{3,2},{4,5},{5,4},{6,7},{7,6},{8,9},{9,8},{10,11... | collective-permute-start | bytes 294920 | tf_op jit(solution)/shard_map/ppermute | solution.py:225
  63.4 5.9 %all-to-all-done.2 = bf16[16,64,128]{2,1,0:T(8,128)(2,1)S(1)} async-done(((bf16[16,64,128]{2,1,0:T(8,128)(2,1)}), bf16[16,64,128]{2,1,0:T(8,128)(2,1)S(1)}, u32[]{:S(2)}, u32[]{:S(2)}) %all-to-all-start.2) | async-done | bytes 262176 | tf_op jit(solution)/shard_map/all_to_all | solution.py:306
  69.3 4.4 %collective-permute-start.5 = (bf16[16,64,128]{2,1,0:T(8,128)(2,1)S(1)}, bf16[16,64,128]{2,1,0:T(8,128)(2,1)S(1)}, u32[]{:S(2)}, u32[]{:S(2)}) collective-permute-start(bf16[16,64,128]{2,1,0:T(8,128)(2,1)S(1)} %all-to-all-done.2), channel_id=1, source_target_pairs={{0,16},{16,0},{1,17},{17,1},{2,18},{18,2},{3,19},{19,3},{4,20},{20... | collective-permute-start | bytes 786440 | tf_op jit(solution)/shard_map/ppermute | solution.py:307
  73.7 0.0 collective-permute-done.8
  73.7 0.0 collective-permute-done.9
  73.7 1.1 %collective-permute-done.5 = bf16[16,64,128]{2,1,0:T(8,128)(2,1)S(1)} collective-permute-done((bf16[16,64,128]{2,1,0:T(8,128)(2,1)S(1)}, bf16[16,64,128]{2,1,0:T(8,128)(2,1)S(1)}, u32[]{:S(2)}, u32[]{:S(2)}) %collective-permute-start.5) | collective-permute-done | bytes 262176 | tf_op jit(solution)/shard_map/ppermute | solution.py:307
  74.8 1.1 %shard_map.71 = (f32[256,768]{1,0:T(8,128)}, f32[256,256]{1,0:T(8,128)}, bf16[4,14,4,256]{3,2,1,0:T(4,128)(2,1)}) custom-call(bf16[8,128,128]{2,1,0:T(8,128)(2,1)S(1)} %bitcast.10, bf16[8,128,128]{2,1,0:T(8,128)(2,1)S(1)} %bitcast.13, f32[4,4,16,256]{3,2,1,0:T(8,128)S(1)} %slice.14.middle, bf16[4,3,16,256]{3,2,1,0:T(8,128)(2,1)S(1)} %get-tuple-element.58.before, ...), custom_call_target="tpu_custom_call" | custom-call | tf_op jit(solution)/shard_map/pallas_call | solution.py:276
  (12 shorter events, 0.4 us)
Async XLA Ops:
  0.6 0.9 %copy-start = (bf16[4,4,14,256]{3,1,2,0:T(4,128)(2,1)S(1)}, bf16[4,4,14,256]{3,1,2,0:T(4,128)(2,1)}, u32[]{:S(2)}) copy-start(bf16[4,4,14,256]{3,1,2,0:T(4,128)(2,1)} %param.4) | copy-start | bytes 344068
  1.5 17.6 %copy-start.1 = (bf16[256,768]{1,0:T(8,128)(2,1)S(1)}, bf16[256,768]{1,0:T(8,128)(2,1)}, u32[]{:S(2)}) copy-start(bf16[256,768]{1,0:T(8,128)(2,1)} %wqkv.5) | copy-start | bytes 1179652
  1.5 17.6 %copy-start.2 = (bf16[256,256]{1,0:T(8,128)(2,1)S(1)}, bf16[256,256]{1,0:T(8,128)(2,1)}, u32[]{:S(2)}) copy-start(bf16[256,256]{1,0:T(8,128)(2,1)} %wout.1) | copy-start | bytes 393220
  1.5 17.6 %copy-start.3 = (bf16[4,4,8,256]{3,2,1,0:T(8,128)(2,1)S(1)}, bf16[4,4,8,256]{3,2,1,0:T(8,128)(2,1)}, u32[]{:S(2)}) copy-start(bf16[4,4,8,256]{3,2,1,0:T(8,128)(2,1)} %cot.3) | copy-start | bytes 196612
  1.6 9.9 %collective-permute-start = (bf16[4,3,16,256]{3,2,1,0:T(8,128)(2,1)S(1)}, bf16[4,3,16,256]{3,2,1,0:T(8,128)(2,1)S(1)}, u32[]{:S(2)}, u32[]{:S(2)}) collective-permute-start(bf16[4,3,16,256]{3,2,1,0:T(8,128)(2,1)S(1)} %get-tuple-element.25), channel_id=1, source_target_pairs={{0,15},{1,2},{2,1},{3,4},{4,3},{5,6},{6,5},{7,8},{8,7},{9,10},{10,... | collective-permute-start | bytes 294920 | tf_op jit(solution)/shard_map/ppermute | solution.py:231
  9.0 4.6 %collective-permute-start.1 = (bf16[4,3,16,256]{3,2,1,0:T(8,128)(2,1)S(1)}, bf16[4,3,16,256]{3,2,1,0:T(8,128)(2,1)S(1)}, u32[]{:S(2)}, u32[]{:S(2)}) collective-permute-start(bf16[4,3,16,256]{3,2,1,0:T(8,128)(2,1)S(1)} %get-tuple-element.26), channel_id=1, source_target_pairs={{0,1},{1,0},{2,3},{3,2},{4,5},{5,4},{6,7},{7,6},{8,9},{9,8},{10,11... | collective-permute-start | bytes 294920 | tf_op jit(solution)/shard_map/ppermute | solution.py:225
  13.8 6.4 %collective-permute-start.2 = (bf16[3,10,16,256]{3,2,1,0:T(8,128)(2,1)S(1)}, bf16[3,10,16,256]{3,2,1,0:T(8,128)(2,1)S(1)}, u32[]{:S(2)}, u32[]{:S(2)}) collective-permute-start(bf16[3,10,16,256]{3,2,1,0:T(8,128)(2,1)S(1)} %get-tuple-element.56), channel_id=1, source_target_pairs={{0,240},{16,32},{32,16},{48,64},{64,48},{80,96},{96,80},{112,128},... | collective-permute-start | bytes 737288 | tf_op jit(solution)/shard_map/ppermute | solution.py:231
  16.3 4.0 %collective-permute-start.3 = (bf16[3,10,16,256]{3,2,1,0:T(8,128)(2,1)S(1)}, bf16[3,10,16,256]{3,2,1,0:T(8,128)(2,1)S(1)}, u32[]{:S(2)}, u32[]{:S(2)}) collective-permute-start(bf16[3,10,16,256]{3,2,1,0:T(8,128)(2,1)S(1)} %get-tuple-element.55), channel_id=1, source_target_pairs={{0,16},{16,0},{32,48},{48,32},{64,80},{80,64},{96,112},{112,96},{1... | collective-permute-start | bytes 737288 | tf_op jit(solution)/shard_map/ppermute | solution.py:225
  23.8 5.3 %collective-permute-start.4 = (bf16[16,64,128]{2,1,0:T(8,128)(2,1)S(1)}, bf16[16,64,128]{2,1,0:T(8,128)(2,1)S(1)}, u32[]{:S(2)}, u32[]{:S(2)}) collective-permute-start(bf16[16,64,128]{2,1,0:T(8,128)(2,1)S(1)} %dynamic-slice_bitcast_fusion), channel_id=1, source_target_pairs={{0,16},{16,0},{1,17},{17,1},{2,18},{18,2},{3,19},{19,3},{4,20},{20... | collective-permute-start | bytes 786440 | tf_op jit(solution)/shard_map/ppermute | solution.py:301
  28.6 7.7 %collective-permute-start.6 = (bf16[3,10,16,256]{3,2,1,0:T(8,128)(2,1)S(1)}, bf16[3,10,16,256]{3,2,1,0:T(8,128)(2,1)S(1)}, u32[]{:S(2)}, u32[]{:S(2)}) collective-permute-start(bf16[3,10,16,256]{3,2,1,0:T(8,128)(2,1)S(1)} %get-tuple-element.49), channel_id=1, source_target_pairs={{0,16},{16,0},{32,48},{48,32},{64,80},{80,64},{96,112},{112,96},{1... | collective-permute-start | bytes 737288 | tf_op jit(solution)/shard_map/ppermute | solution.py:225
  28.7 7.6 %collective-permute-start.7 = (bf16[3,10,16,256]{3,2,1,0:T(8,128)(2,1)S(1)}, bf16[3,10,16,256]{3,2,1,0:T(8,128)(2,1)S(1)}, u32[]{:S(2)}, u32[]{:S(2)}) collective-permute-start(bf16[3,10,16,256]{3,2,1,0:T(8,128)(2,1)S(1)} %get-tuple-element.50), channel_id=1, source_target_pairs={{0,240},{16,32},{32,16},{48,64},{64,48},{80,96},{96,80},{112,128},... | collective-permute-start | bytes 737288 | tf_op jit(solution)/shard_map/ppermute | solution.py:231
  29.9 14.2 %all-to-all-start = ((bf16[16,64,128]{2,1,0:T(8,128)(2,1)}), bf16[16,64,128]{2,1,0:T(8,128)(2,1)S(1)}, u32[]{:S(2)}, u32[]{:S(2)}) async-start(bf16[16,64,128]{2,1,0:T(8,128)(2,1)} %fusion), calls=%async_computation | async-start | bytes 524288 | tf_op jit(solution)/shard_map/all_to_all | solution.py:302
  44.8 12.8 %all-to-all-start.1 = ((bf16[8,64,128]{2,1,0:T(8,128)(2,1)}), bf16[8,64,128]{2,1,0:T(8,128)(2,1)S(1)}, u32[]{:S(2)}, u32[]{:S(2)}) async-start(bf16[8,64,128]{2,1,0:T(8,128)(2,1)} %broadcast_in_dim.4), calls=%async_computation.1 | async-start | bytes 262144 | tf_op jit(solution)/shard_map/all_to_all | solution.py:304
  58.4 10.9 %all-to-all-start.2 = ((bf16[16,64,128]{2,1,0:T(8,128)(2,1)}), bf16[16,64,128]{2,1,0:T(8,128)(2,1)S(1)}, u32[]{:S(2)}, u32[]{:S(2)}) async-start(bf16[16,64,128]{2,1,0:T(8,128)(2,1)} %broadcast_in_dim.5), calls=%async_computation.2 | async-start | bytes 524288 | tf_op jit(solution)/shard_map/all_to_all | solution.py:306
  61.9 11.8 %collective-permute-start.8 = (bf16[4,3,16,256]{3,2,1,0:T(8,128)(2,1)S(1)}, bf16[4,3,16,256]{3,2,1,0:T(8,128)(2,1)S(1)}, u32[]{:S(2)}, u32[]{:S(2)}) collective-permute-start(bf16[4,3,16,256]{3,2,1,0:T(8,128)(2,1)S(1)} %get-tuple-element.54), channel_id=1, source_target_pairs={{0,15},{1,2},{2,1},{3,4},{4,3},{5,6},{6,5},{7,8},{8,7},{9,10},{10,... | collective-permute-start | bytes 294920 | tf_op jit(solution)/shard_map/ppermute | solution.py:231
  62.5 11.2 %collective-permute-start.9 = (bf16[4,3,16,256]{3,2,1,0:T(8,128)(2,1)S(1)}, bf16[4,3,16,256]{3,2,1,0:T(8,128)(2,1)S(1)}, u32[]{:S(2)}, u32[]{:S(2)}) collective-permute-start(bf16[4,3,16,256]{3,2,1,0:T(8,128)(2,1)S(1)} %get-tuple-element.53), channel_id=1, source_target_pairs={{0,1},{1,0},{2,3},{3,2},{4,5},{5,4},{6,7},{7,6},{8,9},{9,8},{10,11... | collective-permute-start | bytes 294920 | tf_op jit(solution)/shard_map/ppermute | solution.py:225
  69.3 5.5 %collective-permute-start.5 = (bf16[16,64,128]{2,1,0:T(8,128)(2,1)S(1)}, bf16[16,64,128]{2,1,0:T(8,128)(2,1)S(1)}, u32[]{:S(2)}, u32[]{:S(2)}) collective-permute-start(bf16[16,64,128]{2,1,0:T(8,128)(2,1)S(1)} %all-to-all-done.2), channel_id=1, source_target_pairs={{0,16},{16,0},{1,17},{17,1},{2,18},{18,2},{3,19},{19,3},{4,20},{20... | collective-permute-start | bytes 786440 | tf_op jit(solution)/shard_map/ppermute | solution.py:307
